TPU v7x, 256 devices: a whole 4x4x8 slice. The times are simulated.
256 devices in a mesh: dp: 8 (over y, core), proto: 32 (over z, x).
Axes of the slice: x: 4, y: 4, z: 8, core: 2. Of those that a mesh axis runs over, the one named last changes fastest.
Arguments:
- student_rows: bfloat16 [128, 256, 256], P('dp'), may hold values from -0.375 to 0.375
- teacher_rows: bfloat16 [128, 256, 256], P('dp'), may hold values from -0.375 to 0.375
- student_proto: bfloat16 [256, 131072], P(None, 'proto'), may hold values from -0.375 to 0.375
- teacher_proto: bfloat16 [256, 131072], P(None, 'proto'), may hold values from -0.375 to 0.375
- center: float32 [131072], P('proto'), may hold values from -0.05 to 0.05
- counts: int32 [128], replicated, may hold values from 1 to 128, 12288 in all
- mask_order: int32 [128, 256], P('dp'), may hold values from 0 to 255, each once within a row
Outputs:
- row_loss: float32 [8, 1536], P('dp')
- student_grad: bfloat16 [8, 1536, 256], P('dp')
Inputs may be any that keep to these rules, and one draw needn't show every extreme that they name: counts sum to 12288, and some image has exactly 128. `mask_order`: each row is a permutation of the patch positions; image i's masked patches are its first counts[i] entries.
All inputs are finite; a program needn't handle non-finite values.
Results may differ from a plain program's by a relative error of at most 0.002.
The roundings to bfloat16 on the way count: a program that leaves them out, or rounds other values in their place, can miss the bound.
Values may be sent and summed in bfloat16 or wider, within the bound.
A program may use at most 192 MiB of HBM per device.

v0:
```python
import jax
import jax.numpy as jnp
from jax import lax
from jax.sharding import PartitionSpec as P

MASK_IMG = 96


STUDENT_TEMP = 0.1
TEACHER_TEMP = 0.07
EPSILON = 1e-06


def norm_columns(weights):
    wide = weights.astype(jnp.float32)
    return (wide / jnp.sqrt(jnp.sum(wide * wide, axis=0, keepdims=True) + EPSILON)).astype(
        jnp.bfloat16
    )


def backward(student_in, student_norm, feature_grad):
    inner = jnp.sum(student_in * feature_grad, axis=-1, keepdims=True)
    return feature_grad / student_norm - student_in * inner / (
        student_norm * student_norm * student_norm
    )


def proto_head(student_part, teacher_part, student_cols, teacher_cols, center):
    student_in = student_part.astype(jnp.float32)
    teacher_in = teacher_part.astype(jnp.float32)
    student_norm = jnp.sqrt(jnp.sum(student_in * student_in, axis=-1, keepdims=True) + EPSILON)
    teacher_norm = jnp.sqrt(jnp.sum(teacher_in * teacher_in, axis=-1, keepdims=True) + EPSILON)
    student_unit = (student_in / student_norm).astype(jnp.bfloat16)
    teacher_unit = (teacher_in / teacher_norm).astype(jnp.bfloat16)
    student_logit = jnp.dot(student_unit, student_cols, preferred_element_type=jnp.float32)
    teacher_logit = jnp.dot(teacher_unit, teacher_cols, preferred_element_type=jnp.float32)
    student_exp = jnp.exp(student_logit / STUDENT_TEMP)
    teacher_exp = jnp.exp((teacher_logit - center[None, :]) / TEACHER_TEMP)
    totals = lax.psum(
        (
            jnp.sum(student_exp, axis=1),
            jnp.sum(teacher_exp, axis=1),
            jnp.sum(teacher_exp * (student_logit / STUDENT_TEMP), axis=1),
        ),
        "proto",
    )
    student_sum, teacher_sum, cross_sum = totals
    row_losses = jnp.log(student_sum) - cross_sum / teacher_sum
    logit_grad = (
        (student_exp / student_sum[:, None] - teacher_exp / teacher_sum[:, None]) / STUDENT_TEMP
    ).astype(jnp.bfloat16)
    feature_grad = lax.dot_general(
        logit_grad, student_cols, (((1,), (1,)), ((), ())), preferred_element_type=jnp.float32
    )
    feature_grad = lax.psum(feature_grad, "proto")
    input_grad = backward(student_in, student_norm, feature_grad)
    return (row_losses, input_grad)


def local(student_rows, teacher_rows, student_proto, teacher_proto, center, counts, mask_order):
    img_dev, patches, feature_width = student_rows.shape
    dp_count = lax.axis_size("dp")
    dp_index = lax.axis_index("dp")
    capacity = img_dev * (patches // 2)
    slot_count = (capacity + dp_count - 1) // dp_count
    mask_dev = MASK_IMG * img_dev
    dev_counts = jnp.sum(counts.reshape(dp_count, img_dev), axis=1)
    dev_ends = jnp.cumsum(dev_counts)
    dev_starts = dev_ends - dev_counts
    is_owner = jnp.arange(dp_count, dtype=jnp.int32) == dp_index
    own_start = jnp.sum(jnp.where(is_owner, dev_starts, 0))
    own_count = jnp.sum(jnp.where(is_owner, dev_counts, 0))
    local_counts = lax.dynamic_slice_in_dim(counts, dp_index * img_dev, img_dev)
    local_ends = jnp.cumsum(local_counts)
    local_starts = local_ends - local_counts
    order_flat = mask_order.reshape(-1)
    targets = jnp.arange(dp_count, dtype=jnp.int32)[:, None]
    slot_ids = jnp.arange(slot_count, dtype=jnp.int32)[None, :]
    send_pos = jnp.mod(targets - own_start, dp_count) + slot_ids * dp_count
    send_valid = send_pos < own_count
    balanced = jnp.arange(mask_dev, dtype=jnp.int32)
    global_pos = balanced * dp_count + dp_index
    source = jnp.sum((global_pos[:, None] >= dev_ends[None, :]).astype(jnp.int32), axis=1)
    source_start = jnp.take(dev_starts, source)
    first_pos = source_start + jnp.mod(dp_index - source_start, dp_count)
    receive_ids = source * slot_count + (global_pos - first_pos) // dp_count
    student_flat = student_rows.reshape(img_dev * patches, feature_width)
    teacher_flat = teacher_rows.reshape(img_dev * patches, feature_width)
    student_cols = norm_columns(student_proto)
    teacher_cols = norm_columns(teacher_proto)
    local_pos = jnp.arange(capacity, dtype=jnp.int32)
    local_valid = (local_pos < own_count)[:, None]
    image_ids = jnp.minimum(
        jnp.sum((local_pos[..., None] >= local_ends).astype(jnp.int32), axis=-1), img_dev - 1
    )
    within = jnp.clip(local_pos - jnp.take(local_starts, image_ids), 0, patches - 1)
    patch_ids = jnp.take(order_flat, image_ids * patches + within)
    local_ids = image_ids * patches + patch_ids
    student_part = jnp.where(local_valid, jnp.take(student_flat, local_ids, axis=0), 0)
    teacher_part = jnp.where(local_valid, jnp.take(teacher_flat, local_ids, axis=0), 0)
    local_losses, local_grad = proto_head(
        student_part, teacher_part, student_cols, teacher_cols, center
    )
    rounded_grad = local_grad.astype(jnp.bfloat16)
    clipped = jnp.clip(send_pos, 0, capacity - 1)
    send_losses = jnp.where(send_valid, jnp.take(local_losses, clipped), 0.0)
    send_grad = jnp.where(
        send_valid[..., None], jnp.take(rounded_grad, clipped, axis=0), jnp.zeros((), jnp.bfloat16)
    )
    got_grad = lax.all_to_all(send_grad, "dp", split_axis=0, concat_axis=0, tiled=True)
    got_losses = lax.all_to_all(send_losses, "dp", split_axis=0, concat_axis=0, tiled=True)
    row_losses = jnp.take(got_losses.reshape(-1), receive_ids)
    input_grad = jnp.take(
        got_grad.reshape(dp_count * slot_count, feature_width), receive_ids, axis=0
    )
    return (row_losses[None, :], input_grad[None])


def solution(mesh):
    placed = (
        P("dp", None, None),
        P("dp", None, None),
        P(None, "proto"),
        P(None, "proto"),
        P("proto"),
        P(),
        P("dp", None),
    )
    return jax.shard_map(
        local,
        mesh=mesh,
        in_specs=placed,
        out_specs=(P("dp", None), P("dp", None, None)),
        check_vma=False,
    )
```

profile of v0, /device:TPU:1, one launch (start us, length us, event | category | flops | bytes accessed | tf_op | source)
XLA Modules:
  0.0 470.4 jit_solution(5885361079008630156)
XLA Ops:
  7.2 0.0 all-reduce.3.cloned.1.call-start
  7.2 0.9 dynamic-slice_bitcast_fusion
  8.1 0.1 copy.11
  8.2 0.1 reduce.2
  8.3 0.7 dynamic-slice_subtract_fusion
  9.1 0.1 convert_reduce_fusion
  9.2 0.7 reshape.739
  9.9 0.7 fusion.50
  10.6 4.4 compare_select_fusion.7
  15.0 0.2 compare_reduce_fusion.8
  15.2 5.7 %select_select_fusion.3 = s32[2048]{0:T(1024)S(1)} fusion(pred[2048]{0:T(1024)(128)(4,1)S(1)} %get-tuple-element.14, pred[2048]{0:T(1024)(128)(4,1)S(1)} %get-tuple-element.12, pred[2048]{0:T(1024)(128)(4,1)S(1)} %get-tuple-element.13, pred[2048]{0:T(1024)(128)(4,1)S(1)} %get-tuple-element.11, pred[2048]{0:T(1024)(128)(4,1)S(1)} %get-tuple-element.10, ...), kind=kLoop, calls=%fused_computation.126 | loop fusion | flops 18432 | bytes 34852 | tf_op jit(solution)/shard_map/jit(_take)/gather | solution.py:96
  21.0 0.7 copy.12
  21.7 11.8 %gather_fusion = s32[2048]{0:T(1024)S(1)} fusion(s32[4096]{0:T(1024)S(1)} %bitcast.50, s32[2048]{0:T(1024)S(1)} %broadcast_clamp_fusion.2), kind=kCustom, calls=%fused_computation.2 | custom fusion | bytes 24576 | tf_op jit(solution)/shard_map/jit(_take)/gather | solution.py:97
  33.6 7.5 %gather_fusion.5 = bf16[2048,256]{1,0:T(8,128)(2,1)S(1)} fusion(bf16[4096,256]{1,0:T(8,128)(2,1)S(1)} %bitcast.48, s32[2048]{0:T(1024)S(1)} %broadcast_clamp_fusion.1), kind=kCustom, calls=%fused_computation.clone | custom fusion | bytes 2105344 | tf_op jit(solution)/shard_map/jit(_take)/gather | solution.py:99
  41.1 10.5 %gather_fusion.6 = bf16[2048,256]{1,0:T(8,128)(2,1)} fusion(bf16[4096,256]{1,0:T(8,128)(2,1)} %bitcast.52, s32[2048]{0:T(1024)S(1)} %broadcast_clamp_fusion.1), kind=kCustom, calls=%fused_computation.1.clone | custom fusion | bytes 2105344 | tf_op jit(solution)/shard_map/jit(_take)/gather | solution.py:100
  51.5 0.1 reduce_sum.121
  51.7 0.2 reduce-window.16
  51.8 1.2 fusion.42
  53.1 0.7 iota_compare_fusion.1
  53.8 0.4 fusion.2
  54.2 2.0 fusion.4
  56.3 1.4 fusion.8
  57.8 0.6 multiply_multiply_fusion
  58.4 13.3 %fusion.17 = f32[2048,4096]{1,0:T(8,128)} fusion(f32[2048]{0:T(1024)S(1)} %get-tuple-element.29, bf16[256,4096]{1,0:T(8,128)(2,1)S(1)} %copy-done.2, f32[4096]{0:T(1024)S(1)} %add_sqrt_fusion.1, bf16[2048,256]{1,0:T(8,128)(2,1)S(1)} %gather_fusion.5, pred[2048]{0:T(1024)(128)(4,1)S(1)} %get-tuple-element.24, pred[2048]{0:T(1024)(128)(4,1)S(1)} %iota_compare_fusion.1), kind=kOutput, calls=%fused_computation.37 | convolution fusion | flops 4300734464 | bytes 36728832 | tf_op jit(solution)/shard_map/dot_general | solution.py:35
  71.7 27.9 %fusion = (f32[2048]{0:T(1024)S(1)}, f32[2048]{0:T(1024)S(1)}, f32[2048]{0:T(1024)S(1)}, f32[2048,4096]{1,0:T(8,128)}) fusion(f32[4096]{0:T(1024)S(1)} %copy-done.10, f32[2048,4096]{1,0:T(8,128)} %fusion.17, bf16[256,4096]{1,0:T(8,128)(2,1)S(1)} %copy-done.5, f32[4096]{0:T(1024)S(1)} %add_sqrt_fusion, f32[2048]{0:T(1024)S(1)} %get-tuple-element.58, ...), kind=kOutput, calls=%fused_computation.11 | convolution fusion | flops 4359448576 | bytes 70324224 | tf_op jit(solution)/shard_map/dot_general | solution.py:36
  99.6 118.9 %all-reduce = (f32[2048]{0:T(1024)S(1)}, f32[2048]{0:T(1024)S(1)}, f32[2048]{0:T(1024)S(1)}) all-reduce(f32[2048]{0:T(1024)S(1)} %get-tuple-element.4, f32[2048]{0:T(1024)S(1)} %get-tuple-element.3, f32[2048]{0:T(1024)S(1)} %get-tuple-element.5), channel_id=1, replica_groups=mesh['dp'=8,'proto'=32] {'proto'}, use_global_device_ids=true, to_apply=%region_14.16 | all-reduce | flops 6144 | bytes 49152 | tf_op jit(solution)/shard_map/psum | solution.py:39
  218.4 26.4 %fusion.1 = f32[2048,256]{1,0:T(8,128)} fusion(f32[2048,4096]{1,0:T(8,128)} %fusion.17, f32[2048,4096]{1,0:T(8,128)} %get-tuple-element.57, f32[2048]{0:T(1024)S(1)} %get-tuple-element.18, f32[2048]{0:T(1024)S(1)} %get-tuple-element.19, f32[4096]{0:T(1024)S(1)} %copy-done.10, bf16[256,4096]{1,0:T(8,128)(2,1)S(1)} %copy-done.2, f32[4096]{0:T(1024)S(1)} %add_sqrt_fusion.1), kind=kOutput, calls=%fused_computation.12 | convolution fusion | flops 4365221888 | bytes 71352320 | tf_op jit(solution)/shard_map/dot_general | solution.py:52
  244.9 0.7 and_select_fusion.9
  245.6 0.1 fusion.29
  245.7 11.8 %gather_fusion.1 = f32[2048]{0:T(1024)S(1)} fusion(f32[2048]{0:T(1024)S(1)} %divide_subtract_fusion, s32[2048]{0:T(1024)S(1)} %broadcast_clamp_fusion), kind=kCustom, calls=%fused_computation.3 | custom fusion | bytes 24576 | tf_op jit(solution)/shard_map/jit(_take)/gather | solution.py:106
  257.5 1.4 compare_select_fusion.13
  258.9 33.0 %all-to-all-start = ((f32[8,1,256]{2,1,0:T(1,128)}), f32[8,1,256]{2,1,0:T(1,128)S(1)}, u32[]{:S(2)}, u32[]{:S(2)}) async-start(f32[8,1,256]{2,1,0:T(1,128)} %compare_select_fusion.13), calls=%async_computation | async-start | bytes 16384 | tf_op jit(solution)/shard_map/all_to_all | solution.py:111
  291.9 0.8 add_compare_fusion
  292.7 124.9 %all-reduce.3.cloned.1.call-done = f32[2048,256]{1,0:T(8,128)} async-done(((f32[2048,256]{1,0:T(8,128)}), f32[2048,256]{1,0:T(8,128)}) %all-reduce.3.cloned.1.call-update) | async-done | bytes 2097168 | tf_op jit(solution)/shard_map/psum | solution.py:55
  417.6 2.4 fusion.12
  420.0 2.0 fusion.15
  422.0 7.5 %gather_fusion.3 = bf16[2048,256]{1,0:T(8,128)(2,1)S(1)} fusion(bf16[2048,256]{1,0:T(8,128)(2,1)S(1)} %fusion.15, s32[2048]{0:T(1024)S(1)} %broadcast_clamp_fusion), kind=kCustom, calls=%fused_computation.5 | custom fusion | bytes 2105344 | tf_op jit(solution)/shard_map/jit(_take)/gather | solution.py:108
  429.5 1.5 select_select_fusion.2
  431.1 9.6 %all-to-all-start.1 = ((bf16[8,256,256]{2,1,0:T(8,128)(2,1)}), bf16[8,256,256]{2,1,0:T(8,128)(2,1)S(1)}, u32[]{:S(2)}, u32[]{:S(2)}) async-start(bf16[8,256,256]{2,1,0:T(8,128)(2,1)} %select_select_fusion.2), calls=%async_computation.1 | async-start | bytes 2097152 | tf_op jit(solution)/shard_map/all_to_all | solution.py:110
  440.7 0.1 convert_reduce_fusion.1
  440.9 0.7 fusion.49
  441.6 4.4 fusion.36
  446.0 0.7 compare_and_fusion.1
  446.7 0.1 fusion.37
  446.8 8.4 %gather_fusion.2 = f32[1536]{0:T(1024)S(1)} fusion(f32[2048]{0:T(1024)S(1)} %bitcast.49, s32[2048]{0:T(1024)S(1)} %pad_clamp_fusion), kind=kCustom, calls=%fused_computation.4 | custom fusion | bytes 18432 | tf_op jit(solution)/shard_map/jit(_take)/gather | solution.py:112
  455.2 0.7 and_select_fusion.5
  455.9 5.4 %gather_fusion.4 = bf16[1536,256]{1,0:T(8,128)(2,1)} fusion(bf16[2048,256]{1,0:T(8,128)(2,1)S(1)} %bitcast.51, s32[2048]{0:T(1024)S(1)} %pad_clamp_fusion), kind=kCustom, calls=%fused_computation.6 | custom fusion | bytes 1579008 | tf_op jit(solution)/shard_map/jit(_take)/gather | solution.py:113
  461.3 2.3 bitcast_select_fusion
  (40 shorter events, 0.3 us)
Async XLA Ops:
  7.2 26.4 %copy-start = (bf16[16,256,256]{2,1,0:T(8,128)(2,1)S(1)}, bf16[16,256,256]{2,1,0:T(8,128)(2,1)}, u32[]{:S(2)}) copy-start(bf16[16,256,256]{2,1,0:T(8,128)(2,1)} %param.9) | copy-start | bytes 6291460
  7.2 410.4 %all-reduce.3.cloned.1.call-start = ((), (), s32[]{:S(2)}) async-start(), calls=%async_computation.2 | async-start | bytes 4194304 | tf_op jit(solution)/shard_map/psum | solution.py:55
  41.1 12.7 %copy-start.2 = (bf16[256,4096]{1,0:T(8,128)(2,1)S(1)}, bf16[256,4096]{1,0:T(8,128)(2,1)}, u32[]{:S(2)}) copy-start(bf16[256,4096]{1,0:T(8,128)(2,1)} %param.11) | copy-start | bytes 6291460
  51.8 5.9 %copy-start.8 = (s32[8,1]{0,1:T(1,128)}, s32[8,1]{0,1:T(1,128)S(1)}, u32[]{:S(2)}) copy-start(s32[8,1]{0,1:T(1,128)S(1)} %reduce-window.16) | copy-start | bytes 100
  51.8 4.5 copy-start.4
  58.4 13.3 %copy-start.5 = (bf16[256,4096]{1,0:T(8,128)(2,1)S(1)}, bf16[256,4096]{1,0:T(8,128)(2,1)}, u32[]{:S(2)}) copy-start(bf16[256,4096]{1,0:T(8,128)(2,1)} %param.12) | copy-start | bytes 6291460
  58.4 13.3 %copy-start.10 = (f32[4096]{0:T(1024)S(1)}, f32[4096]{0:T(1024)}, u32[]{:S(2)}) copy-start(f32[4096]{0:T(1024)} %param.13) | copy-start | bytes 49156
  245.7 174.3 %copy-start.7 = (f32[2048]{0:T(1024)S(1)}, f32[2048]{0:T(1024)}, u32[]{:S(2)}) copy-start(f32[2048]{0:T(1024)} %get-tuple-element.28) | copy-start | bytes 24580
  258.9 172.2 %all-to-all-start = ((f32[8,1,256]{2,1,0:T(1,128)}), f32[8,1,256]{2,1,0:T(1,128)S(1)}, u32[]{:S(2)}, u32[]{:S(2)}) async-start(f32[8,1,256]{2,1,0:T(1,128)} %compare_select_fusion.13), calls=%async_computation | async-start | bytes 16384 | tf_op jit(solution)/shard_map/all_to_all | solution.py:111
  417.6 2.4 copy-start.3
  429.5 11.2 %copy-start.9 = (s32[8,1]{0,1:T(1,128)S(1)}, s32[8,1]{0,1:T(1,128)}, u32[]{:S(2)}) copy-start(s32[8,1]{0,1:T(1,128)} %copy-done.8) | copy-start | bytes 100
  429.5 11.3 %copy-start.6 = (s32[8]{0:T(128)S(1)}, s32[8]{0:T(128)}, u32[]{:S(2)}) copy-start(s32[8]{0:T(128)} %get-tuple-element.23) | copy-start | bytes 100
  431.1 24.8 %all-to-all-start.1 = ((bf16[8,256,256]{2,1,0:T(8,128)(2,1)}), bf16[8,256,256]{2,1,0:T(8,128)(2,1)S(1)}, u32[]{:S(2)}, u32[]{:S(2)}) async-start(bf16[8,256,256]{2,1,0:T(8,128)(2,1)} %select_select_fusion.2), calls=%async_computation.1 | async-start | bytes 2097152 | tf_op jit(solution)/shard_map/all_to_all | solution.py:110
  455.9 7.6 %copy-start.1 = (bf16[16,256,256]{2,1,0:T(8,128)(2,1)S(1)}, bf16[16,256,256]{2,1,0:T(8,128)(2,1)}, u32[]{:S(2)}) copy-start(bf16[16,256,256]{2,1,0:T(8,128)(2,1)} %param.9) | copy-start | bytes 6291460
Sparse Core Ops, SparseCore 0:
  245.0 172.5 all-reduce.2
where the time goes:
time: 471 us; the launch traced here: 470 us
  waiting for transfers between devices  125 us (27%)
  blocking collectives  119 us (25%)
  matrix products  67.6 us (14%)
  local copies, waits for them, and re-layouts  66.6 us (14%)
  starting transfers between devices  42.7 us (9%)
  other arithmetic  35.3 us (7%)
  between operations  14.4 us (3%)
    psum x1, waiting for transfers between devices, proto_head(): feature_grad = lax.psum(feature_grad, 'proto')  125 us
    psum x1, blocking collectives, proto_head(): lax.psum((jnp.sum(student_exp, axis=1), jnp.sum(teacher_exp, axis=1), jnp...  119 us
    all_to_all x1, starting transfers between devices, local(): lax.all_to_all(send_losses, 'dp', split_axis=0, concat_axis=0, tiled=True)  33 us
    dot_general x1, matrix products, proto_head(): jnp.dot(teacher_unit, teacher_cols, preferred_element_type=jnp.float32)  27.9 us
    dot_general x1, matrix products, proto_head(): lax.dot_general(logit_grad, student_cols, (((1,), (1,)), ((), ())), prefe...  26.4 us
    dot_general x1, matrix products, proto_head(): jnp.dot(student_unit, student_cols, preferred_element_type=jnp.float32)  13.3 us
    gather x1, local copies, waits for them, and re-layouts, local(): patch_ids = jnp.take(order_flat, image_ids * patches + within)  11.8 us
    gather x1, local copies, waits for them, and re-layouts, local(): send_losses = jnp.where(send_valid, jnp.take(local_losses, clipped), 0.0)  11.8 us
  transfers between devices with their start and end apart: 3, of which 1 were waited for; matrix products, arithmetic and copies ran while one was open for 9% of the time, Pallas kernels for 0%

commit v1 on v0

v1 whole, which is shorter than its diff:
```python
import functools
import math

import jax
import jax.numpy as jnp
from jax import lax
from jax.experimental import pallas as pl
from jax.experimental.pallas import tpu as pltpu
from jax.sharding import PartitionSpec as P

STUDENT_TEMP = 0.1
TEACHER_TEMP = 0.07
EPSILON = 1e-06
LOG2E = math.log2(math.e)
X_SIZE = 4
F32 = jnp.float32
BF16 = jnp.bfloat16
MESH = pl.DeviceIdType.MESH
NT = (((1,), (1,)), ((), ()))
TN = (((0,), (0,)), ((), ()))


def iota(shape, dim):
    return lax.broadcasted_iota(jnp.int32, shape, dim)


def head_kernel(dims, *refs):
    ndp, nz, nx, images, slots, block = dims
    (student_hbm, teacher_hbm, sproto_hbm, tproto_hbm, center_ref, counts_ref, order_ref,
     gathered, losses,
     scols, scols_t, tcols_t, center_b, s_in, s_unit, t_unit, stat_x, stat_z, grad_x, got_x, grad_z, got_z, own_dp, got_dp,
     load_sem, sx_send, sx_recv, sz_send, sz_recv, gx_send, gx_recv, gz_send, gz_recv,
     dp_send, dp_recv, az_send, az_recv, ax_send, ax_recv, lo_send, lo_recv) = refs
    chunks = images // nx
    rows = nx * slots
    piece = slots // nz
    per_res = piece // ndp
    slot_rows = own_dp.shape[2]
    protos = scols.shape[1]
    width = scols.shape[0]
    patches = order_ref.shape[1]
    me = lax.axis_index("dp")
    q = lax.axis_index("proto")
    z = q // nx
    x = q % nx

    def along_x(d):
        return (me, z * nx + lax.rem(x + d, nx))

    def along_z(d):
        return (me, lax.rem(z + d, nz) * nx + x)

    def along_dp(d):
        return (lax.rem(me + d, ndp), q)

    barrier = pltpu.get_barrier_semaphore()
    partners = (
        [along_x(d) for d in range(1, nx)]
        + [along_z(d) for d in range(1, nz)]
        + [along_dp(d) for d in range(1, ndp)]
    )
    for partner in partners:
        pl.semaphore_signal(barrier, inc=1, device_id=partner, device_id_type=MESH)

    def prologue(srows, trows, tcols):
        loads = [
            pltpu.make_async_copy(src, dst, load_sem.at[i])
            for i, (src, dst) in enumerate(
                ((student_hbm, srows), (teacher_hbm, trows), (sproto_hbm, scols), (tproto_hbm, tcols))
            )
        ]
        for load in loads:
            load.start()

        def spread_center(n, carry):
            at = pl.ds(pl.multiple_of(n * 128, 128), 128)
            row = center_ref[:, at] * (LOG2E / TEACHER_TEMP)
            center_b[at, :] = jnp.transpose(jnp.broadcast_to(row, (128, 128)))
            return carry

        lax.fori_loop(0, protos // 128, spread_center, 0)
        loads[0].wait()
        loads[1].wait()

        def gather_image(i, carry):
            order = order_ref[pl.ds(i, 1), :][:, :slots]
            pick = (iota((patches, slots), 0) == order).astype(F32).astype(BF16)
            student = lax.dot_general(pick, srows[i], TN, preferred_element_type=F32)
            teacher = lax.dot_general(pick, trows[i], TN, preferred_element_type=F32)
            at = pl.ds(pl.multiple_of(i * slots, slots), slots)
            s_in[i] = student.astype(BF16)
            s_norm = jnp.sqrt(jnp.sum(student * student, axis=1, keepdims=True) + EPSILON)
            t_norm = jnp.sqrt(jnp.sum(teacher * teacher, axis=1, keepdims=True) + EPSILON)
            s_unit[at, :] = (student / s_norm).astype(BF16)
            t_unit[at, :] = (teacher / t_norm).astype(BF16)
            return carry

        lax.fori_loop(0, images, gather_image, 0)
        loads[2].wait()
        loads[3].wait()

        def norm_tile(n, carry):
            at = pl.ds(pl.multiple_of(n * 256, 256), 256)
            for cols, turned in ((scols, scols_t), (tcols, tcols_t)):
                wide = cols[:, at].astype(F32)
                scale = 1.0 / jnp.sqrt(jnp.sum(wide * wide, axis=0, keepdims=True) + EPSILON)
                unit = (wide * scale).astype(BF16)
                if cols is scols:
                    cols[:, at] = unit
                turned[at, :] = jnp.transpose(unit)
            return carry

        lax.fori_loop(0, protos // 256, norm_tile, 0)

    pl.run_scoped(
        prologue,
        pltpu.VMEM((images, patches, width), BF16),
        pltpu.VMEM((images, patches, width), BF16),
        pltpu.VMEM((width, protos), BF16),
    )

    def copy(src, dst, send, recv, device):
        return pltpu.make_async_remote_copy(
            src_ref=src, dst_ref=dst, send_sem=send, recv_sem=recv, device_id=device,
            device_id_type=MESH,
        )

    def stat_x_copy(c, d):
        return copy(stat_x.at[c, 0], stat_x.at[c, d], sx_send.at[c, d], sx_recv.at[c, d], along_x(d))

    def stat_z_copy(c, d):
        return copy(stat_z.at[c, 0], stat_z.at[c, d], sz_send.at[c, d], sz_recv.at[c, d], along_z(d))

    def grad_x_copy(c, d):
        return copy(
            grad_x.at[c, lax.rem(x + d, nx)], got_x.at[c, d], gx_send.at[c, d], gx_recv.at[c, d],
            along_x(d),
        )

    def grad_z_copy(c, d):
        return copy(
            grad_z.at[c, lax.rem(z + d, nz)], got_z.at[c, d], gz_send.at[c, d], gz_recv.at[c, d],
            along_z(d),
        )

    def dp_copy(c, d):
        return copy(
            own_dp.at[c, lax.rem(me + d, ndp)], got_dp.at[c, me], dp_send.at[c, d], dp_recv.at[c, d],
            along_dp(d),
        )

    def all_z_copy(c, d):
        block_ref = gathered.at[x, c, z]
        return copy(block_ref, block_ref, az_send.at[c, d], az_recv.at[c, d], along_z(d))

    def all_x_copy(c, d):
        block_ref = gathered.at[x, c]
        return copy(block_ref, block_ref, ax_send.at[c, d], ax_recv.at[c, d], along_x(d))

    def loss_copy(d):
        return copy(losses.at[me], losses.at[me], lo_send.at[d], lo_recv.at[d], along_dp(d))

    def statistics(s_exp, t_exp, c):
        slot = lax.rem(c, 2)
        at_rows = pl.ds(pl.multiple_of(c * rows, rows), rows)
        student = s_unit[at_rows, :]
        teacher = t_unit[at_rows, :]

        sums = [jnp.zeros((8, rows), F32)] * 3
        for n in range(0, protos, block):
            at = pl.ds(n, block)
            s = lax.dot_general(scols_t[at, :], student, NT, preferred_element_type=F32)
            t = lax.dot_general(tcols_t[at, :], teacher, NT, preferred_element_type=F32)
            shift = jnp.concatenate([center_b[at, :]] * (rows // 128), axis=1)
            es = jnp.exp2(s * (LOG2E / STUDENT_TEMP))
            et = jnp.exp2(t * (LOG2E / TEACHER_TEMP) - shift)
            s_exp[slot, at, :] = es
            t_exp[slot, at, :] = et
            sums = [
                total + jnp.sum(part.reshape(block // 8, 8, rows), axis=0)
                for total, part in zip(sums, (es, et, et * s))
            ]
        lines = [jnp.sum(total, axis=0, keepdims=True) for total in sums]
        stat_x[c, 0] = jnp.concatenate(lines + [jnp.zeros((1, rows), F32)], axis=0)
        for d in range(1, nx):
            stat_x_copy(c, d).start()

    def statistics_over_z(c):
        total = stat_x[c, 0]
        for d in range(1, nx):
            stat_x_copy(c, d).wait_recv()
            total = total + stat_x[c, d]
        stat_z[c, 0] = total
        for d in range(1, nz):
            stat_z_copy(c, d).start()

    def gradient(s_exp, t_exp, c):
        slot = lax.rem(c, 2)
        total = stat_z[c, 0]
        for d in range(1, nz):
            stat_z_copy(c, d).wait_recv()
            total = total + stat_z[c, d]
        s_sum, t_sum, cross = total[0:1, :], total[1:2, :], total[2:3, :]
        loss = jnp.log(s_sum) - cross * (1.0 / STUDENT_TEMP) / t_sum
        losses[me, pl.ds(c * nx, nx), :] = jnp.concatenate(
            [loss[:, i * slots : (i + 1) * slots] for i in range(nx)], axis=0
        )
        s_scale = (1.0 / STUDENT_TEMP) / s_sum
        t_scale = (1.0 / STUDENT_TEMP) / t_sum
        dz = jnp.zeros((width, rows), F32)
        for n in range(0, protos, block):
            at = pl.ds(n, block)
            dlogit = (s_exp[slot, at, :] * s_scale - t_exp[slot, at, :] * t_scale).astype(BF16)
            dz = dz + jnp.dot(scols[:, at], dlogit, preferred_element_type=F32)
        grad_x[c] = jnp.transpose(dz).reshape(nx, slots, width)
        for d in range(1, nx):
            grad_x_copy(c, d).start()

    def gradient_over_z(c):
        total = grad_x[c, x]
        for d in range(1, nx):
            grad_x_copy(c, d).wait_recv()
            total = total + got_x[c, d]
        grad_z[c] = total.reshape(nz, piece, width)
        for d in range(1, nz):
            grad_z_copy(c, d).start()

    def finish(c):
        dz = grad_z[c, z]
        for d in range(1, nz):
            grad_z_copy(c, d).wait_recv()
            dz = dz + got_z[c, d]
        image = c * nx + x
        xs = s_in[image, pl.ds(pl.multiple_of(z * piece, piece), piece), :].astype(F32)
        norm = jnp.sqrt(jnp.sum(xs * xs, axis=1, keepdims=True) + EPSILON)
        inner = jnp.sum(xs * dz, axis=1, keepdims=True)
        dx = (dz / norm - xs * inner / (norm * norm * norm)).astype(BF16)
        before = iota(counts_ref.shape, 1) < me * images + image
        start = jnp.sum(jnp.where(before, counts_ref[...].astype(F32), 0.0), axis=1, keepdims=True)
        first = jnp.broadcast_to(start.astype(jnp.int32), (ndp * slot_rows, piece))
        pos = iota((ndp * slot_rows, piece), 0)
        k = iota((ndp * slot_rows, piece), 1)
        pick = (((first + k) % ndp) == pos // slot_rows) & (k // ndp == pos % slot_rows)
        sent = jnp.dot(pick.astype(F32).astype(BF16), dx, preferred_element_type=F32)
        own_dp[c] = sent.reshape(ndp, slot_rows, width)
        for d in range(1, ndp):
            dp_copy(c, d).start()
        got_dp[c, me] = own_dp[c, me]

    def spread_z(c):
        for d in range(1, ndp):
            dp_copy(c, d).wait_recv()
        held = got_dp[c].reshape(ndp * slot_rows, width).astype(BF16)
        pos = iota((piece, ndp * slot_rows), 0)
        k = iota((piece, ndp * slot_rows), 1)
        pick = (k // slot_rows == pos // per_res) & (k % slot_rows == pos % per_res)
        gathered[x, c, z] = jnp.dot(
            pick.astype(F32).astype(BF16), held, preferred_element_type=F32
        ).astype(BF16)
        for d in range(1, nz):
            all_z_copy(c, d).start()

    def spread_x(c):
        for d in range(1, nz):
            all_z_copy(c, d).wait_recv()
        for d in range(1, nx):
            all_x_copy(c, d).start()

    pl.semaphore_wait(barrier, len(partners))

    def pipeline(s_exp, t_exp):
        def step(t, carry):
            def at_lag(lag, work):
                c = t - lag

                @pl.when((c >= 0) & (c < chunks))
                def _():
                    work(c)

            at_lag(0, functools.partial(statistics, s_exp, t_exp))
            at_lag(2, gradient_over_z)
            at_lag(1, functools.partial(gradient, s_exp, t_exp))
            at_lag(0, statistics_over_z)
            at_lag(3, finish)
            at_lag(4, spread_z)
            at_lag(5, spread_x)
            return carry

        lax.fori_loop(0, chunks + 5, step, 0)

    pl.run_scoped(
        pipeline,
        pltpu.VMEM((2, protos, rows), F32),
        pltpu.VMEM((2, protos, rows), F32),
    )
    for d in range(1, ndp):
        loss_copy(d).start()

    def drain(c, carry):
        for d in range(1, nx):
            all_x_copy(c, d).wait_recv()
            stat_x_copy(c, d).wait_send()
            grad_x_copy(c, d).wait_send()
            all_x_copy(c, d).wait_send()
        for d in range(1, nz):
            stat_z_copy(c, d).wait_send()
            grad_z_copy(c, d).wait_send()
            all_z_copy(c, d).wait_send()
        for d in range(1, ndp):
            dp_copy(c, d).wait_send()
        return carry

    lax.fori_loop(0, chunks, drain, 0)
    for d in range(1, ndp):
        loss_copy(d).wait()


def place_kernel(dims, gathered, losses, counts_ref, row_loss, grad):
    ndp, nz, nx, images, slots, tile = dims
    chunks = images // nx
    piece = slots // nz
    per_res = piece // ndp
    total_images = counts_ref.shape[1]
    me = lax.axis_index("dp")
    counts = counts_ref[...].astype(F32)
    upto = (iota((total_images, total_images), 0) <= iota((total_images, total_images), 1))
    ends = jnp.dot(
        jnp.broadcast_to(counts, (8, total_images)).astype(BF16), upto.astype(F32).astype(BF16),
        preferred_element_type=F32,
    )[0:1, :]
    starts = (ends - counts).astype(jnp.int32)
    ends = ends.astype(jnp.int32)
    b = pl.program_id(0) * tile + iota((tile, 1), 0)
    g = b * ndp + me
    image = jnp.sum((g >= ends).astype(F32), axis=1, keepdims=True).astype(jnp.int32)
    start = jnp.max(jnp.where(g >= starts, starts, 0).astype(F32), axis=1, keepdims=True)
    j = g - start.astype(jnp.int32)
    owner, own_image = image // images, image % images
    at = ((own_image % nx) * chunks + own_image // nx) * nz + j // piece
    at = at * piece + owner * per_res + (j % piece) // ndp
    held = gathered.shape[0]
    pick = (iota((tile, held), 1) == at).astype(F32).astype(BF16)
    grad[...] = jnp.dot(pick, gathered[...], preferred_element_type=F32).astype(BF16)
    wide = losses[...]
    high = wide.astype(BF16)
    rest = wide - high.astype(F32)
    middle = rest.astype(BF16)
    low = (rest - middle.astype(F32)).astype(BF16)
    pick_image = (iota((tile, total_images), 1) == image).astype(F32).astype(BF16)
    lines = sum(
        jnp.dot(pick_image, part, preferred_element_type=F32) for part in (low, middle, high)
    )
    lines = jnp.where(iota((tile, slots), 1) == j, lines, 0.0)
    row_loss[...] = jnp.sum(jnp.transpose(lines), axis=0, keepdims=True)


def local(ndp, nz, nx, student_rows, teacher_rows, student_proto, teacher_proto, center, counts, order):
    images, patches, width = student_rows.shape
    slots = patches // 2
    protos = student_proto.shape[1]
    chunks = images // nx
    rows = nx * slots
    piece = slots // nz
    slot_rows = max(8, piece // ndp)
    block = min(512, protos)
    mask_dev = counts.shape[0] * 96 // ndp
    dims = (ndp, nz, nx, images, slots, block)
    any_spec = pl.BlockSpec(memory_space=pl.ANY)
    vmem = pl.BlockSpec(memory_space=pltpu.VMEM)
    counts = counts[None, :]
    dma = pltpu.SemaphoreType.DMA
    gathered, losses = pl.pallas_call(
        functools.partial(head_kernel, dims),
        out_shape=(
            jax.ShapeDtypeStruct((nx, chunks, nz, piece, width), BF16),
            jax.ShapeDtypeStruct((ndp, images, slots), F32),
        ),
        in_specs=[any_spec] * 4 + [vmem] * 3,
        out_specs=(vmem, vmem),
        scratch_shapes=[
            pltpu.VMEM((width, protos), BF16),
            pltpu.VMEM((protos, width), BF16),
            pltpu.VMEM((protos, width), BF16),
            pltpu.VMEM((protos, 128), F32),
            pltpu.VMEM((images, slots, width), BF16),
            pltpu.VMEM((images * slots, width), BF16),
            pltpu.VMEM((images * slots, width), BF16),
            pltpu.VMEM((chunks, nx, 4, rows), F32),
            pltpu.VMEM((chunks, nz, 4, rows), F32),
            pltpu.VMEM((chunks, nx, slots, width), F32),
            pltpu.VMEM((chunks, nx, slots, width), F32),
            pltpu.VMEM((chunks, nz, piece, width), F32),
            pltpu.VMEM((chunks, nz, piece, width), F32),
            pltpu.VMEM((chunks, ndp, slot_rows, width), F32),
            pltpu.VMEM((chunks, ndp, slot_rows, width), F32),
            dma((4,)),
            dma((chunks, nx)), dma((chunks, nx)),
            dma((chunks, nz)), dma((chunks, nz)),
            dma((chunks, nx)), dma((chunks, nx)),
            dma((chunks, nz)), dma((chunks, nz)),
            dma((chunks, ndp)), dma((chunks, ndp)),
            dma((chunks, nz)), dma((chunks, nz)),
            dma((chunks, nx)), dma((chunks, nx)),
            dma((ndp,)), dma((ndp,)),
        ],
        compiler_params=pltpu.CompilerParams(
            collective_id=0, has_side_effects=True, vmem_limit_bytes=63 * 2**20
        ),
        name="proto_head",
    )(student_rows, teacher_rows, student_proto, teacher_proto, center[None, :], counts, order)
    tile = 256 if mask_dev % 256 == 0 else 128
    held = nx * chunks * nz * piece
    row_loss, grad = pl.pallas_call(
        functools.partial(place_kernel, (ndp, nz, nx, images, slots, tile)),
        grid=(mask_dev // tile,),
        out_shape=(
            jax.ShapeDtypeStruct((1, mask_dev), F32),
            jax.ShapeDtypeStruct((mask_dev, width), BF16),
        ),
        in_specs=[
            pl.BlockSpec((held, width), lambda i: (0, 0)),
            pl.BlockSpec((ndp * images, slots), lambda i: (0, 0)),
            pl.BlockSpec((1, ndp * images), lambda i: (0, 0)),
        ],
        out_specs=(
            pl.BlockSpec((1, tile), lambda i: (0, i)),
            pl.BlockSpec((tile, width), lambda i: (i, 0)),
        ),
        compiler_params=pltpu.CompilerParams(vmem_limit_bytes=32 * 2**20),
        name="place_rows",
    )(gathered.reshape(held, width), losses.reshape(ndp * images, slots), counts)
    return row_loss, grad[None]


def solution(mesh):
    ndp, proto = mesh.shape["dp"], mesh.shape["proto"]
    nx = X_SIZE
    placed = (
        P("dp", None, None),
        P("dp", None, None),
        P(None, "proto"),
        P(None, "proto"),
        P("proto"),
        P(),
        P("dp", None),
    )
    return jax.shard_map(
        functools.partial(local, ndp, proto // nx, nx),
        mesh=mesh,
        in_specs=placed,
        out_specs=(P("dp", None), P("dp", None, None)),
        check_vma=False,
    )
```

time: 471 us -> 99.6 us (0.21)
  waiting for transfers between devices: 125 us -> 0 us
  blocking collectives: 119 us -> 0 us
  Pallas kernels: 0 us -> 96.6 us
  matrix products: 67.6 us -> 0 us
  local copies, waits for them, and re-layouts: 66.6 us -> 2.06 us
  starting transfers between devices: 42.7 us -> 0 us
  other arithmetic: 35.3 us -> 0 us
  between operations: 14.4 us -> 0.67 us
    psum x1 -> x0, waiting for transfers between devices: 125 us -> none  [proto_head(): feature_grad = lax.psum(feature_grad, 'proto')]
    psum x1 -> x0, blocking collectives: 119 us -> none  [proto_head(): lax.psum((jnp.sum(student_exp, axis=1), jnp.sum(teacher_exp, axis=1), jnp...]
    pallas_call x0 -> x2, Pallas kernels: none -> 96.6 us  [the longest x1 89.3 us: local(): pl.pallas_call(functools.partial(head_kernel, dims), out_shape=(jax.Shape...]
    dot_general x3 -> x0, matrix products: 67.6 us -> none  [the longest x1 27.9 us: proto_head(): jnp.dot(teacher_unit, teacher_cols, preferred_element_type=jnp.float32)]
    gather x9 -> x0, local copies, waits for them, and re-layouts: 64.2 us -> none  [the longest x1 11.8 us: local(): patch_ids = jnp.take(order_flat, image_ids * patches + within)]
    all_to_all x2 -> x0, starting transfers between devices: 42.7 us -> none  [the longest x1 33 us: local(): lax.all_to_all(send_losses, 'dp', split_axis=0, concat_axis=0, tiled=True)]
    gather x9 -> x0, other arithmetic: 14.8 us -> none  [the longest x3 10.3 us: local(): jnp.take(local_starts, image_ids)]
    reduce_sum x8 -> x0, other arithmetic: 7.84 us -> none  [the longest x2 2.47 us: norm_columns(): jnp.sum(wide * wide, axis=0, keepdims=True) + EPSILON]
  transfers between devices with their start and end apart: 3 -> 0, of which waited for: 1 -> 0; matrix products, arithmetic and copies ran while one was open for 9% -> 0% of each run, Pallas kernels for 0% -> 0%
where the time goes in v1:
time: 99.6 us; the launch traced here: 99.3 us
  Pallas kernels  96.6 us (97%)
  local copies, waits for them, and re-layouts  2.06 us (2%)
    pallas_call x1, Pallas kernels, local(): pl.pallas_call(functools.partial(head_kernel, dims), out_shape=(jax.Shape...  89.3 us
    pallas_call x1, Pallas kernels, local(): pl.pallas_call(functools.partial(place_kernel, (ndp, nz, nx, images, slot...  7.35 us
    unnamed x6, local copies, waits for them, and re-layouts  2.06 us

profile of v1, /device:TPU:1, one launch (start us, length us, event | category | flops | bytes accessed | tf_op | source)
XLA Modules:
  0.0 99.3 jit_solution(4985827583424979603)
XLA Ops:
  0.6 0.0 copy-start.2
  0.6 89.3 %proto_head.1 = (bf16[4,4,8,16,256]{4,3,2,1,0:T(8,128)(2,1)}, f32[8,16,128]{2,1,0:T(8,128)}) custom-call(bf16[16,256,256]{2,1,0:T(8,128)(2,1)} %refs_0_.1, bf16[16,256,256]{2,1,0:T(8,128)(2,1)} %refs_1_.1, bf16[256,4096]{1,0:T(8,128)(2,1)} %refs_2_.1, bf16[256,4096]{1,0:T(8,128)(2,1)} %refs_3_.1, f32[1,4096]{1,0:T(1,128)} %bitcast.9, s32[1,128]{1,0:T(1,128)} %bitcast.7, ...), custom_call_target="tpu_custom_call" | custom-call | tf_op jit(solution)/shard_map/proto_head/pallas_call | solution.py:372
  89.9 0.0 copy-done.2
  89.9 0.0 copy-start
  89.9 1.2 %copy-done = bf16[4,4,8,16,256]{4,3,2,1,0:T(8,128)(2,1)S(1)} copy-done((bf16[4,4,8,16,256]{4,3,2,1,0:T(8,128)(2,1)S(1)}, bf16[4,4,8,16,256]{4,3,2,1,0:T(8,128)(2,1)}, u32[]{:S(2)}) %copy-start) | copy-done | bytes 1048600
  91.2 0.0 copy-start.1
  91.2 0.8 copy-done.1
  92.0 7.3 %place_rows.1 = (f32[1,1536]{1,0:T(1,128)}, bf16[1536,256]{1,0:T(8,128)(2,1)}) custom-call(bf16[2048,256]{1,0:T(8,128)(2,1)S(1)} %bitcast.5, f32[128,128]{1,0:T(8,128)S(1)} %bitcast.6, s32[1,128]{1,0:T(1,128)S(1)} %bitcast.8), custom_call_target="tpu_custom_call" | custom-call | tf_op jit(solution)/shard_map/place_rows/pallas_call | solution.py:413
Async XLA Ops:
  0.6 89.3 %copy-start.2 = (s32[128]{0:T(128)S(1)}, s32[128]{0:T(128)}, u32[]{:S(2)}) copy-start(s32[128]{0:T(128)} %param.12) | copy-start | bytes 1540
  89.9 1.2 %copy-start = (bf16[4,4,8,16,256]{4,3,2,1,0:T(8,128)(2,1)S(1)}, bf16[4,4,8,16,256]{4,3,2,1,0:T(8,128)(2,1)}, u32[]{:S(2)}) copy-start(bf16[4,4,8,16,256]{4,3,2,1,0:T(8,128)(2,1)} %get-tuple-element.6) | copy-start | bytes 3145732
  91.2 0.8 copy-start.1

commit v2 on v1

v2 whole, which is shorter than its diff:
```python
import functools
import math

import jax
import jax.numpy as jnp
from jax import lax
from jax.experimental import pallas as pl
from jax.experimental.pallas import tpu as pltpu
from jax.sharding import PartitionSpec as P

STUDENT_TEMP = 0.1
TEACHER_TEMP = 0.07
EPSILON = 1e-06
LOG2E = math.log2(math.e)
X_SIZE = 4
HALVES = 2
DEPTH = 4
F32 = jnp.float32
BF16 = jnp.bfloat16
MESH = pl.DeviceIdType.MESH
NT = (((1,), (1,)), ((), ()))
TN = (((0,), (0,)), ((), ()))


def iota(shape, dim):
    return lax.broadcasted_iota(jnp.int32, shape, dim)


def head_kernel(dims, *refs):
    ndp, nz, nx, images, slots, block, tile = dims
    (student_hbm, teacher_hbm, sproto_hbm, tproto_hbm, center_ref, counts_ref, order_ref,
     row_loss, grad,
     scols, scols_t, tcols_t, center_b, s_in, s_unit, t_unit, stat_x, stat_z, grad_x, got_x,
     grad_z, got_z, own_dp, got_dp, gathered, losses, row_at,
     load_sem, sx_send, sx_recv, sz_send, sz_recv, gx_send, gx_recv, gz_send, gz_recv,
     dp_send, dp_recv, az_send, az_recv, ax_send, ax_recv, lo_send, lo_recv) = refs
    chunks = images // nx
    units = chunks * HALVES
    half = slots // HALVES
    rows = nx * half
    piece = slots // nz
    unit_piece = half // nz
    per_res = piece // ndp
    slot_rows = own_dp.shape[2]
    protos = scols.shape[1]
    width = scols.shape[0]
    patches = order_ref.shape[1]
    total_images = counts_ref.shape[1]
    mask_dev = grad.shape[0]
    held = nx * nz * piece
    me = lax.axis_index("dp")
    q = lax.axis_index("proto")
    z = q // nx
    x = q % nx

    def along_x(d):
        return (me, z * nx + lax.rem(x + d, nx))

    def along_z(d):
        return (me, lax.rem(z + d, nz) * nx + x)

    def along_dp(d):
        return (lax.rem(me + d, ndp), q)

    barrier = pltpu.get_barrier_semaphore()
    partners = (
        [along_x(d) for d in range(1, nx)]
        + [along_z(d) for d in range(1, nz)]
        + [along_dp(d) for d in range(1, ndp)]
    )
    for partner in partners:
        pl.semaphore_signal(barrier, inc=1, device_id=partner, device_id_type=MESH)

    def prologue(srows, trows, tcols):
        loads = [
            pltpu.make_async_copy(src, dst, load_sem.at[i])
            for i, (src, dst) in enumerate(
                ((student_hbm, srows), (teacher_hbm, trows), (sproto_hbm, scols), (tproto_hbm, tcols))
            )
        ]
        for load in loads:
            load.start()

        def spread_center(n, carry):
            for i in range(256 // 128):
                at = pl.ds(pl.multiple_of(n * 256 + i * 128, 128), 128)
                row = center_ref[:, at] * (LOG2E / TEACHER_TEMP)
                center_b[at, :] = jnp.transpose(jnp.broadcast_to(row, (128, 128)))
            return carry

        def gather_chunk(c, carry):
            for i in range(nx):
                image = c * nx + i
                order = order_ref[pl.ds(image, 1), :][:, :slots]
                pick = (iota((patches, slots), 0) == order).astype(F32).astype(BF16)
                for source, units_ref in ((srows, s_unit), (trows, t_unit)):
                    wide = lax.dot_general(pick, source[image], TN, preferred_element_type=F32)
                    if source is srows:
                        s_in[image] = wide.astype(BF16)
                    norm = jnp.sqrt(jnp.sum(wide * wide, axis=1, keepdims=True) + EPSILON)
                    unit = (wide / norm).reshape(nz, HALVES, unit_piece, width)
                    for h in range(HALVES):
                        units_ref[c * HALVES + h, i] = unit[:, h].reshape(half, width).astype(BF16)
            return carry

        def norm_tiles(n, carry):
            for i in range(group):
                at = pl.ds(pl.multiple_of((n * group + i) * 256, 256), 256)
                for cols, turned in ((scols, scols_t), (tcols, tcols_t)):
                    wide = cols[:, at].astype(F32)
                    scale = 1.0 / jnp.sqrt(jnp.sum(wide * wide, axis=0, keepdims=True) + EPSILON)
                    unit = (wide * scale).astype(BF16)
                    if cols is scols:
                        cols[:, at] = unit
                    turned[at, :] = jnp.transpose(unit)
            return carry

        group = min(4, protos // 256)
        lax.fori_loop(0, protos // 256, spread_center, 0)
        loads[0].wait()
        loads[1].wait()
        lax.fori_loop(0, chunks, gather_chunk, 0)
        loads[2].wait()
        loads[3].wait()
        lax.fori_loop(0, protos // (256 * group), norm_tiles, 0)

    pl.run_scoped(
        prologue,
        pltpu.VMEM((images, patches, width), BF16),
        pltpu.VMEM((images, patches, width), BF16),
        pltpu.VMEM((width, protos), BF16),
    )

    def copy(src, dst, send, recv, device):
        return pltpu.make_async_remote_copy(
            src_ref=src, dst_ref=dst, send_sem=send, recv_sem=recv, device_id=device,
            device_id_type=MESH,
        )

    def stat_x_copy(c, d):
        return copy(stat_x.at[c, 0], stat_x.at[c, d], sx_send.at[c, d], sx_recv.at[c, d], along_x(d))

    def stat_z_copy(c, d):
        return copy(stat_z.at[c, 0], stat_z.at[c, d], sz_send.at[c, d], sz_recv.at[c, d], along_z(d))

    def grad_x_copy(c, d):
        return copy(
            grad_x.at[c, lax.rem(x + d, nx)], got_x.at[c, d], gx_send.at[c, d], gx_recv.at[c, d],
            along_x(d),
        )

    def grad_z_copy(c, d):
        return copy(
            grad_z.at[c, lax.rem(z + d, nz)], got_z.at[c, d], gz_send.at[c, d], gz_recv.at[c, d],
            along_z(d),
        )

    def dp_copy(c, d):
        return copy(
            own_dp.at[c, lax.rem(me + d, ndp)], got_dp.at[c, me], dp_send.at[c, d], dp_recv.at[c, d],
            along_dp(d),
        )

    def all_z_copy(c, d):
        block_ref = gathered.at[c, x, z]
        return copy(block_ref, block_ref, az_send.at[c, d], az_recv.at[c, d], along_z(d))

    def all_x_copy(c, d):
        block_ref = gathered.at[c, x]
        return copy(block_ref, block_ref, ax_send.at[c, d], ax_recv.at[c, d], along_x(d))

    def loss_copy(d):
        return copy(losses.at[me], losses.at[me], lo_send.at[d], lo_recv.at[d], along_dp(d))

    def statistics(s_exp, t_exp, c):
        slot = lax.rem(c, DEPTH)
        student = s_unit[c].reshape(rows, width)
        teacher = t_unit[c].reshape(rows, width)
        sums = [jnp.zeros((8, rows), F32)] * 3
        for n in range(0, protos, block):
            at = pl.ds(n, block)
            s = lax.dot_general(scols_t[at, :], student, NT, preferred_element_type=F32)
            t = lax.dot_general(tcols_t[at, :], teacher, NT, preferred_element_type=F32)
            shift = jnp.concatenate([center_b[at, :]] * (rows // 128), axis=1)
            es = jnp.exp2(s * (LOG2E / STUDENT_TEMP))
            et = jnp.exp2(t * (LOG2E / TEACHER_TEMP) - shift)
            s_exp[slot, at, :] = es
            t_exp[slot, at, :] = et
            sums = [
                total + jnp.sum(part.reshape(block // 8, 8, rows), axis=0)
                for total, part in zip(sums, (es, et, et * s))
            ]
        lines = [jnp.sum(total, axis=0, keepdims=True) for total in sums]
        stat_x[c, 0] = jnp.concatenate(lines + [jnp.zeros((1, rows), F32)], axis=0)
        for d in range(1, nx):
            stat_x_copy(c, d).start()

    def statistics_over_z(c):
        total = stat_x[c, 0]
        for d in range(1, nx):
            stat_x_copy(c, d).wait_recv()
            total = total + stat_x[c, d]
        stat_z[c, 0] = total
        for d in range(1, nz):
            stat_z_copy(c, d).start()

    def gradient(s_exp, t_exp, c):
        slot = lax.rem(c, DEPTH)
        total = stat_z[c, 0]
        for d in range(1, nz):
            stat_z_copy(c, d).wait_recv()
            total = total + stat_z[c, d]
        s_sum, t_sum, cross = total[0:1, :], total[1:2, :], total[2:3, :]
        loss = jnp.log(s_sum) - cross * (1.0 / STUDENT_TEMP) / t_sum
        losses[me, pl.ds(c, 1), :] = loss
        s_scale = (1.0 / STUDENT_TEMP) / s_sum
        t_scale = (1.0 / STUDENT_TEMP) / t_sum
        dz = jnp.zeros((width, rows), F32)
        for n in range(0, protos, block):
            at = pl.ds(n, block)
            dlogit = (s_exp[slot, at, :] * s_scale - t_exp[slot, at, :] * t_scale).astype(BF16)
            dz = dz + jnp.dot(scols[:, at], dlogit, preferred_element_type=F32)
        grad_x[c] = jnp.transpose(dz).reshape(nx, half, width)
        for d in range(1, nx):
            grad_x_copy(c, d).start()

    def gradient_over_z(c):
        total = grad_x[c, x]
        for d in range(1, nx):
            grad_x_copy(c, d).wait_recv()
            total = total + got_x[c, d]
        grad_z[c] = total.reshape(nz, unit_piece, width)
        for d in range(1, nz):
            grad_z_copy(c, d).start()

    def finish(c):
        parts = []
        for h in range(HALVES):
            u = c * HALVES + h
            part = grad_z[u, z]
            for d in range(1, nz):
                grad_z_copy(u, d).wait_recv()
                part = part + got_z[u, d]
            parts.append(part)
        dz = jnp.concatenate(parts, axis=0)
        image = c * nx + x
        xs = s_in[image, pl.ds(pl.multiple_of(z * piece, piece), piece), :].astype(F32)
        norm = jnp.sqrt(jnp.sum(xs * xs, axis=1, keepdims=True) + EPSILON)
        inner = jnp.sum(xs * dz, axis=1, keepdims=True)
        dx = (dz / norm - xs * inner / (norm * norm * norm)).astype(BF16)
        before = iota(counts_ref.shape, 1) < me * images + image
        start = jnp.sum(jnp.where(before, counts_ref[...].astype(F32), 0.0), axis=1, keepdims=True)
        first = jnp.broadcast_to(start.astype(jnp.int32), (ndp * slot_rows, piece))
        pos = iota((ndp * slot_rows, piece), 0)
        k = iota((ndp * slot_rows, piece), 1)
        pick = (((first + k) % ndp) == pos // slot_rows) & (k // ndp == pos % slot_rows)
        sent = jnp.dot(pick.astype(F32).astype(BF16), dx, preferred_element_type=F32)
        own_dp[c] = sent.reshape(ndp, slot_rows, width)
        for d in range(1, ndp):
            dp_copy(c, d).start()
        got_dp[c, me] = own_dp[c, me]

    def spread_z(c):
        for d in range(1, ndp):
            dp_copy(c, d).wait_recv()
        held = got_dp[c].reshape(ndp * slot_rows, width).astype(BF16)
        pos = iota((piece, ndp * slot_rows), 0)
        k = iota((piece, ndp * slot_rows), 1)
        pick = (k // slot_rows == pos // per_res) & (k % slot_rows == pos % per_res)
        gathered[c, x, z] = jnp.dot(
            pick.astype(F32).astype(BF16), held, preferred_element_type=F32
        ).astype(BF16)
        for d in range(1, nz):
            all_z_copy(c, d).start()

    def spread_x(c):
        for d in range(1, nz):
            all_z_copy(c, d).wait_recv()
        for d in range(1, nx):
            all_x_copy(c, d).start()

    def row_of(n):
        counts = counts_ref[...].astype(F32)
        upto = iota((total_images, total_images), 0) <= iota((total_images, total_images), 1)
        ends = jnp.dot(
            jnp.broadcast_to(counts, (8, total_images)).astype(BF16),
            upto.astype(F32).astype(BF16), preferred_element_type=F32,
        )[0:1, :]
        starts = ends - counts
        g = (n * tile + iota((tile, 1), 0)) * ndp + me
        wide = g.astype(F32)
        image = jnp.sum((wide >= ends).astype(F32), axis=1, keepdims=True).astype(jnp.int32)
        start = jnp.max(jnp.where(wide >= starts, starts, 0.0), axis=1, keepdims=True)
        return image // images, image % images, g - start.astype(jnp.int32)

    def index_rows():
        for n in range(mask_dev // tile):
            owner, image, j = row_of(n)
            at = image * nz + j // piece
            at = at * piece + owner * per_res + (j % piece) // ndp
            row_at[n * tile : (n + 1) * tile, :] = jnp.broadcast_to(at, (tile, 128))
        grad[...] = jnp.zeros_like(grad)

    def place(c):
        for d in range(1, nx):
            all_x_copy(c, d).wait_recv()
        values = gathered[c].reshape(held, width)
        for n in range(mask_dev // tile):
            at = jnp.concatenate([row_at[n * tile : (n + 1) * tile, :]] * (held // 128), axis=1)
            pick = (iota((tile, held), 1) + c * held == at).astype(F32).astype(BF16)
            put = jnp.dot(pick, values, preferred_element_type=F32)
            lines = slice(n * tile, (n + 1) * tile)
            grad[lines, :] = (grad[lines, :].astype(F32) + put).astype(BF16)

    def send_losses():
        for d in range(1, ndp):
            loss_copy(d).start()

    def place_losses():
        for d in range(1, ndp):
            loss_copy(d).wait_recv()
        wide = losses[...].reshape(ndp * units, rows)
        high = wide.astype(BF16)
        rest = wide - high.astype(F32)
        middle = rest.astype(BF16)
        low = (rest - middle.astype(F32)).astype(BF16)
        for n in range(mask_dev // tile):
            owner, image, j = row_of(n)
            line = owner * units + (image // nx) * HALVES + (j // unit_piece) % HALVES
            lane = (image % nx) * half + (j // piece) * unit_piece + j % unit_piece
            pick = (iota((tile, ndp * units), 1) == line).astype(F32).astype(BF16)
            lines = sum(
                jnp.dot(pick, part, preferred_element_type=F32) for part in (low, middle, high)
            )
            lines = jnp.where(iota((tile, rows), 1) == lane, lines, 0.0)
            row_loss[:, n * tile : (n + 1) * tile] = jnp.sum(
                jnp.transpose(lines), axis=0, keepdims=True
            )

    pl.semaphore_wait(barrier, len(partners))

    def pipeline(s_exp, t_exp):
        def step(t, carry):
            def at_lag(lag, work, every=1):
                u = t - lag

                @pl.when((u >= 0) & (u < units) & (lax.rem(u, every) == every - 1))
                def _():
                    work(u // every)

            at_lag(0, functools.partial(statistics, s_exp, t_exp))
            at_lag(1, statistics_over_z)
            at_lag(DEPTH - 1, functools.partial(gradient, s_exp, t_exp))

            @pl.when(t == units + DEPTH - 2)
            def _():
                send_losses()
                index_rows()

            at_lag(5, gradient_over_z)
            at_lag(6, finish, HALVES)
            at_lag(7, spread_z, HALVES)
            at_lag(8, spread_x, HALVES)

            @pl.when(t == units + DEPTH)
            def _():
                place_losses()

            at_lag(9, place, HALVES)
            return carry

        lax.fori_loop(0, units + 9, step, 0)

    pl.run_scoped(
        pipeline,
        pltpu.VMEM((DEPTH, protos, rows), F32),
        pltpu.VMEM((DEPTH, protos, rows), F32),
    )
    def drain_unit(u, carry):
        for d in range(1, nx):
            stat_x_copy(u, d).wait_send()
            grad_x_copy(u, d).wait_send()
        for d in range(1, nz):
            stat_z_copy(u, d).wait_send()
            grad_z_copy(u, d).wait_send()
        return carry

    def drain_chunk(c, carry):
        for d in range(1, nx):
            all_x_copy(c, d).wait_send()
        for d in range(1, nz):
            all_z_copy(c, d).wait_send()
        for d in range(1, ndp):
            dp_copy(c, d).wait_send()
        return carry

    lax.fori_loop(0, units, drain_unit, 0)
    lax.fori_loop(0, chunks, drain_chunk, 0)
    for d in range(1, ndp):
        loss_copy(d).wait_send()


def local(ndp, nz, nx, student_rows, teacher_rows, student_proto, teacher_proto, center, counts, order):
    images, patches, width = student_rows.shape
    slots = patches // 2
    protos = student_proto.shape[1]
    chunks = images // nx
    units = chunks * HALVES
    half = slots // HALVES
    rows = nx * half
    piece = slots // nz
    slot_rows = max(8, piece // ndp)
    mask_dev = counts.shape[0] * 96 // ndp
    tile = 256 if mask_dev % 256 == 0 else 128
    dims = (ndp, nz, nx, images, slots, min(512, protos), tile)
    any_spec = pl.BlockSpec(memory_space=pl.ANY)
    vmem = pl.BlockSpec(memory_space=pltpu.VMEM)
    dma = pltpu.SemaphoreType.DMA
    row_loss, grad = pl.pallas_call(
        functools.partial(head_kernel, dims),
        out_shape=(
            jax.ShapeDtypeStruct((1, mask_dev), F32),
            jax.ShapeDtypeStruct((mask_dev, width), BF16),
        ),
        in_specs=[any_spec] * 4 + [vmem] * 3,
        out_specs=(vmem, vmem),
        scratch_shapes=[
            pltpu.VMEM((width, protos), BF16),
            pltpu.VMEM((protos, width), BF16),
            pltpu.VMEM((protos, width), BF16),
            pltpu.VMEM((protos, 128), F32),
            pltpu.VMEM((images, slots, width), BF16),
            pltpu.VMEM((units, nx, half, width), BF16),
            pltpu.VMEM((units, nx, half, width), BF16),
            pltpu.VMEM((units, nx, 4, rows), F32),
            pltpu.VMEM((units, nz, 4, rows), F32),
            pltpu.VMEM((units, nx, half, width), F32),
            pltpu.VMEM((units, nx, half, width), F32),
            pltpu.VMEM((units, nz, half // nz, width), F32),
            pltpu.VMEM((units, nz, half // nz, width), F32),
            pltpu.VMEM((chunks, ndp, slot_rows, width), F32),
            pltpu.VMEM((chunks, ndp, slot_rows, width), F32),
            pltpu.VMEM((chunks, nx, nz, piece, width), BF16),
            pltpu.VMEM((ndp, units, rows), F32),
            pltpu.VMEM((mask_dev, 128), jnp.int32),
            dma((4,)),
            dma((units, nx)), dma((units, nx)),
            dma((units, nz)), dma((units, nz)),
            dma((units, nx)), dma((units, nx)),
            dma((units, nz)), dma((units, nz)),
            dma((chunks, ndp)), dma((chunks, ndp)),
            dma((chunks, nz)), dma((chunks, nz)),
            dma((chunks, nx)), dma((chunks, nx)),
            dma((ndp,)), dma((ndp,)),
        ],
        compiler_params=pltpu.CompilerParams(
            collective_id=0, has_side_effects=True, vmem_limit_bytes=63 * 2**20
        ),
        name="proto_head",
    )(student_rows, teacher_rows, student_proto, teacher_proto, center[None, :], counts[None, :], order)
    return row_loss, grad[None]


def solution(mesh):
    ndp, proto = mesh.shape["dp"], mesh.shape["proto"]
    nx = X_SIZE
    placed = (
        P("dp", None, None),
        P("dp", None, None),
        P(None, "proto"),
        P(None, "proto"),
        P("proto"),
        P(),
        P("dp", None),
    )
    return jax.shard_map(
        functools.partial(local, ndp, proto // nx, nx),
        mesh=mesh,
        in_specs=placed,
        out_specs=(P("dp", None), P("dp", None, None)),
        check_vma=False,
    )
```

time: 99.6 us -> 90.6 us (0.910)
  Pallas kernels: 96.6 us -> 86.4 us
  local copies, waits for them, and re-layouts: 2.06 us -> 3.35 us
    pallas_call x1 -> x0, Pallas kernels: 7.35 us -> none  [local(): pl.pallas_call(functools.partial(place_kernel, (ndp, nz, nx, images, slot...]
    pallas_call x1, Pallas kernels: 89.3 us -> 86.4 us  [local(): pl.pallas_call(functools.partial(head_kernel, dims), out_shape=(jax.Shape...]
    unnamed x6 -> x2, local copies, waits for them, and re-layouts: 2.06 us -> 3.35 us
where the time goes in v2:
time: 90.6 us; the launch traced here: 90.4 us
  Pallas kernels  86.4 us (95%)
  local copies, waits for them, and re-layouts  3.35 us (4%)
    pallas_call x1, Pallas kernels, local(): pl.pallas_call(functools.partial(head_kernel, dims), out_shape=(jax.Shape...  86.4 us
    unnamed x2, local copies, waits for them, and re-layouts  3.35 us

profile of v2, /device:TPU:1, one launch (start us, length us, event | category | flops | bytes accessed | tf_op | source)
XLA Modules:
  0.0 90.4 jit_solution(800800448463107520)
XLA Ops:
  0.6 86.4 %proto_head.1 = (f32[1,1536]{1,0:T(1,128)}, bf16[1536,256]{1,0:T(8,128)(2,1)}) custom-call(bf16[16,256,256]{2,1,0:T(8,128)(2,1)} %refs_0_.1, bf16[16,256,256]{2,1,0:T(8,128)(2,1)} %refs_1_.1, bf16[256,4096]{1,0:T(8,128)(2,1)} %refs_2_.1, bf16[256,4096]{1,0:T(8,128)(2,1)} %refs_3_.1, f32[1,4096]{1,0:T(1,128)} %bitcast.4, s32[1,128]{1,0:T(1,128)} %bitcast.5, ...), custom_call_target="tpu_custom_call" | custom-call | tf_op jit(solution)/shard_map/proto_head/pallas_call | solution.py:419
  87.0 1.3 %copy.11 = f32[1,1536]{1,0:T(1,128)} copy(f32[1,1536]{1,0:T(1,128)} %get-tuple-element.8) | data formatting | bytes 12288
  88.3 2.1 %copy.12 = bf16[1,1536,256]{2,1,0:T(8,128)(2,1)} copy(bf16[1,1536,256]{2,1,0:T(8,128)(2,1)} %bitcast.3) | data formatting | bytes 1572864

commit v3 on v2

--- a/solution.py
+++ b/solution.py
@@ -31,7 +31,7 @@
     (student_hbm, teacher_hbm, sproto_hbm, tproto_hbm, center_ref, counts_ref, order_ref,
      row_loss, grad,
      scols, scols_t, tcols_t, center_b, s_in, s_unit, t_unit, stat_x, stat_z, grad_x, got_x,
-     grad_z, got_z, own_dp, got_dp, gathered, losses, row_at,
+     grad_z, got_z, own_dp, got_dp, gathered, losses, row_at, row_key,
      load_sem, sx_send, sx_recv, sz_send, sz_recv, gx_send, gx_recv, gz_send, gz_recv,
      dp_send, dp_recv, az_send, az_recv, ax_send, ax_recv, lo_send, lo_recv) = refs
     chunks = images // nx
@@ -115,14 +115,16 @@
                     turned[at, :] = jnp.transpose(unit)
             return carry
 
-        group = min(4, protos // 256)
+        group = protos // 256 // chunks
+
+        def prepare(c, carry):
+            gather_chunk(c, carry)
+            return norm_tiles(c, carry)
+
         lax.fori_loop(0, protos // 256, spread_center, 0)
-        loads[0].wait()
-        loads[1].wait()
-        lax.fori_loop(0, chunks, gather_chunk, 0)
-        loads[2].wait()
-        loads[3].wait()
-        lax.fori_loop(0, protos // (256 * group), norm_tiles, 0)
+        for load in loads:
+            load.wait()
+        lax.fori_loop(0, chunks, prepare, 0)
 
     pl.run_scoped(
         prologue,
@@ -279,7 +281,7 @@
         for d in range(1, nx):
             all_x_copy(c, d).start()
 
-    def row_of(n):
+    def index_rows():
         counts = counts_ref[...].astype(F32)
         upto = iota((total_images, total_images), 0) <= iota((total_images, total_images), 1)
         ends = jnp.dot(
@@ -287,30 +289,39 @@
             upto.astype(F32).astype(BF16), preferred_element_type=F32,
         )[0:1, :]
         starts = ends - counts
-        g = (n * tile + iota((tile, 1), 0)) * ndp + me
-        wide = g.astype(F32)
-        image = jnp.sum((wide >= ends).astype(F32), axis=1, keepdims=True).astype(jnp.int32)
-        start = jnp.max(jnp.where(wide >= starts, starts, 0.0), axis=1, keepdims=True)
-        return image // images, image % images, g - start.astype(jnp.int32)
-
-    def index_rows():
-        for n in range(mask_dev // tile):
-            owner, image, j = row_of(n)
-            at = image * nz + j // piece
-            at = at * piece + owner * per_res + (j % piece) // ndp
-            row_at[n * tile : (n + 1) * tile, :] = jnp.broadcast_to(at, (tile, 128))
+
+        def index_tile(n, carry):
+            g = (n * tile + iota((tile, 1), 0)) * ndp + me
+            wide = g.astype(F32)
+            image = jnp.sum((wide >= ends).astype(F32), axis=1, keepdims=True).astype(jnp.int32)
+            start = jnp.max(jnp.where(wide >= starts, starts, 0.0), axis=1, keepdims=True)
+            j = g - start.astype(jnp.int32)
+            owner, image = image // images, image % images
+            at = (image * nz + j // piece) * piece + owner * per_res + (j % piece) // ndp
+            lines = pl.ds(pl.multiple_of(n * tile, tile), tile)
+            row_at[lines, :] = jnp.broadcast_to(at, (tile, 128))
+            line = owner * units + (image // nx) * HALVES + (j // unit_piece) % HALVES
+            lane = (image % nx) * half + (j // piece) * unit_piece + j % unit_piece
+            row_key[lines, :] = jnp.broadcast_to(line * rows + lane, (tile, 128))
+            return carry
+
+        lax.fori_loop(0, mask_dev // tile, index_tile, 0)
         grad[...] = jnp.zeros_like(grad)
 
     def place(c):
         for d in range(1, nx):
             all_x_copy(c, d).wait_recv()
         values = gathered[c].reshape(held, width)
-        for n in range(mask_dev // tile):
-            at = jnp.concatenate([row_at[n * tile : (n + 1) * tile, :]] * (held // 128), axis=1)
-            pick = (iota((tile, held), 1) + c * held == at).astype(F32).astype(BF16)
+
+        def place_tile(n, carry):
+            lines = pl.ds(pl.multiple_of(n * tile, tile), tile)
+            at = jnp.concatenate([row_at[lines, :] - c * held] * (held // 128), axis=1)
+            pick = (iota((tile, held), 1) == at).astype(F32).astype(BF16)
             put = jnp.dot(pick, values, preferred_element_type=F32)
-            lines = slice(n * tile, (n + 1) * tile)
             grad[lines, :] = (grad[lines, :].astype(F32) + put).astype(BF16)
+            return carry
+
+        lax.fori_loop(0, mask_dev // tile, place_tile, 0)
 
     def send_losses():
         for d in range(1, ndp):
@@ -324,14 +335,15 @@
         rest = wide - high.astype(F32)
         middle = rest.astype(BF16)
         low = (rest - middle.astype(F32)).astype(BF16)
+
         for n in range(mask_dev // tile):
-            owner, image, j = row_of(n)
-            line = owner * units + (image // nx) * HALVES + (j // unit_piece) % HALVES
-            lane = (image % nx) * half + (j // piece) * unit_piece + j % unit_piece
-            pick = (iota((tile, ndp * units), 1) == line).astype(F32).astype(BF16)
+            key = row_key[n * tile : (n + 1) * tile, :]
+            line, lane = key // rows, key % rows
+            pick = (iota((tile, 128), 1) == line).astype(F32).astype(BF16)[:, : ndp * units]
             lines = sum(
                 jnp.dot(pick, part, preferred_element_type=F32) for part in (low, middle, high)
             )
+            lane = jnp.concatenate([lane] * (rows // 128), axis=1)
             lines = jnp.where(iota((tile, rows), 1) == lane, lines, 0.0)
             row_loss[:, n * tile : (n + 1) * tile] = jnp.sum(
                 jnp.transpose(lines), axis=0, keepdims=True
@@ -348,34 +360,46 @@
                 def _():
                     work(u // every)
 
+            @pl.when(t == DEPTH)
+            def _():
+                index_rows()
+
+            at_lag(DEPTH, functools.partial(gradient, s_exp, t_exp))
+            at_lag(1, statistics_over_z)
             at_lag(0, functools.partial(statistics, s_exp, t_exp))
-            at_lag(1, statistics_over_z)
-            at_lag(DEPTH - 1, functools.partial(gradient, s_exp, t_exp))
-
-            @pl.when(t == units + DEPTH - 2)
-            def _():
-                send_losses()
-                index_rows()
-
-            at_lag(5, gradient_over_z)
-            at_lag(6, finish, HALVES)
-            at_lag(7, spread_z, HALVES)
-            at_lag(8, spread_x, HALVES)
-
-            @pl.when(t == units + DEPTH)
-            def _():
-                place_losses()
-
-            at_lag(9, place, HALVES)
-            return carry
-
-        lax.fori_loop(0, units + 9, step, 0)
+            at_lag(DEPTH + 2, gradient_over_z)
+            at_lag(DEPTH + 3, finish, HALVES)
+            at_lag(DEPTH + 4, spread_z, HALVES)
+            return carry
+
+        lax.fori_loop(0, units + DEPTH, step, 0)
 
     pl.run_scoped(
         pipeline,
         pltpu.VMEM((DEPTH, protos, rows), F32),
         pltpu.VMEM((DEPTH, protos, rows), F32),
     )
+    def each(first, last, work):
+        def one(c, carry):
+            work(c)
+            return carry
+
+        lax.fori_loop(first, last, one, 0)
+
+    last = chunks - 1
+    send_losses()
+    finish(last - 1)
+    each(units - 2, units, gradient_over_z)
+    spread_z(last - 1)
+    each(0, last - 1, spread_x)
+    finish(last)
+    place_losses()
+    spread_x(last - 1)
+    spread_z(last)
+    each(0, last - 1, place)
+    spread_x(last)
+    each(last - 1, chunks, place)
+
     def drain_unit(u, carry):
         for d in range(1, nx):
             stat_x_copy(u, d).wait_send()
@@ -443,6 +467,7 @@
             pltpu.VMEM((chunks, nx, nz, piece, width), BF16),
             pltpu.VMEM((ndp, units, rows), F32),
             pltpu.VMEM((mask_dev, 128), jnp.int32),
+            pltpu.VMEM((mask_dev, 128), jnp.int32),
             dma((4,)),
             dma((units, nx)), dma((units, nx)),
             dma((units, nz)), dma((units, nz)),

time: 90.6 us -> 104 us (1.15)
  Pallas kernels: 86.4 us -> 99.8 us
    pallas_call x1, Pallas kernels: 86.4 us -> 99.8 us  [local(): pl.pallas_call(functools.partial(head_kernel, dims), out_shape=(jax.Shape...]
where the time goes in v3:
time: 104 us
  Pallas kernels  99.8 us (96%)
  local copies, waits for them, and re-layouts  3.35 us (3%)
    pallas_call x1, Pallas kernels, local(): pl.pallas_call(functools.partial(head_kernel, dims), out_shape=(jax.Shape...  99.8 us
    unnamed x2, local copies, waits for them, and re-layouts  3.35 us

profile of v3, /device:TPU:1, one launch (start us, length us, event | category | flops | bytes accessed | tf_op | source)
XLA Modules:
  0.0 103.7 jit_solution(5697311645903365037)
XLA Ops:
  0.6 99.8 %proto_head.1 = (f32[1,1536]{1,0:T(1,128)}, bf16[1536,256]{1,0:T(8,128)(2,1)}) custom-call(bf16[16,256,256]{2,1,0:T(8,128)(2,1)} %refs_0_.1, bf16[16,256,256]{2,1,0:T(8,128)(2,1)} %refs_1_.1, bf16[256,4096]{1,0:T(8,128)(2,1)} %refs_2_.1, bf16[256,4096]{1,0:T(8,128)(2,1)} %refs_3_.1, f32[1,4096]{1,0:T(1,128)} %bitcast.4, s32[1,128]{1,0:T(1,128)} %bitcast.5, ...), custom_call_target="tpu_custom_call" | custom-call | tf_op jit(solution)/shard_map/proto_head/pallas_call | solution.py:443
  100.4 1.3 %copy.11 = f32[1,1536]{1,0:T(1,128)} copy(f32[1,1536]{1,0:T(1,128)} %get-tuple-element.8) | data formatting | bytes 12288
  101.7 2.1 %copy.12 = bf16[1,1536,256]{2,1,0:T(8,128)(2,1)} copy(bf16[1,1536,256]{2,1,0:T(8,128)(2,1)} %bitcast.3) | data formatting | bytes 1572864

commit v4 on v3

--- a/solution.py
+++ b/solution.py
@@ -140,39 +140,43 @@
         )
 
     def stat_x_copy(c, d):
-        return copy(stat_x.at[c, 0], stat_x.at[c, d], sx_send.at[c, d], sx_recv.at[c, d], along_x(d))
+        return copy(stat_x.at[c, 0], stat_x.at[c, d], sx_send, sx_recv.at[c], along_x(d))
 
     def stat_z_copy(c, d):
-        return copy(stat_z.at[c, 0], stat_z.at[c, d], sz_send.at[c, d], sz_recv.at[c, d], along_z(d))
+        return copy(stat_z.at[c, 0], stat_z.at[c, d], sz_send, sz_recv.at[c], along_z(d))
 
     def grad_x_copy(c, d):
         return copy(
-            grad_x.at[c, lax.rem(x + d, nx)], got_x.at[c, d], gx_send.at[c, d], gx_recv.at[c, d],
-            along_x(d),
+            grad_x.at[c, lax.rem(x + d, nx)], got_x.at[c, d], gx_send, gx_recv.at[c], along_x(d)
         )
 
     def grad_z_copy(c, d):
         return copy(
-            grad_z.at[c, lax.rem(z + d, nz)], got_z.at[c, d], gz_send.at[c, d], gz_recv.at[c, d],
-            along_z(d),
+            grad_z.at[c, lax.rem(z + d, nz)], got_z.at[c, d], gz_send, gz_recv.at[c], along_z(d)
         )
 
-    def dp_copy(c, d):
+    def dp_copy(batch, d):
+        n, at = batch
         return copy(
-            own_dp.at[c, lax.rem(me + d, ndp)], got_dp.at[c, me], dp_send.at[c, d], dp_recv.at[c, d],
+            own_dp.at[lax.rem(me + d, ndp), at], got_dp.at[me, at], dp_send, dp_recv.at[n],
             along_dp(d),
         )
 
-    def all_z_copy(c, d):
-        block_ref = gathered.at[c, x, z]
-        return copy(block_ref, block_ref, az_send.at[c, d], az_recv.at[c, d], along_z(d))
-
-    def all_x_copy(c, d):
-        block_ref = gathered.at[c, x]
-        return copy(block_ref, block_ref, ax_send.at[c, d], ax_recv.at[c, d], along_x(d))
+    def all_z_copy(batch, d):
+        n, at = batch
+        block_ref = gathered.at[at, x, z]
+        return copy(block_ref, block_ref, az_send, az_recv.at[n], along_z(d))
+
+    def all_x_copy(batch, d):
+        n, at = batch
+        block_ref = gathered.at[at, x]
+        return copy(block_ref, block_ref, ax_send, ax_recv.at[n], along_x(d))
 
     def loss_copy(d):
-        return copy(losses.at[me], losses.at[me], lo_send.at[d], lo_recv.at[d], along_dp(d))
+        return copy(losses.at[me], losses.at[me], lo_send, lo_recv, along_dp(d))
+
+    def await_bytes(ref, sem):
+        pltpu.make_async_copy(ref, ref, sem).wait()
 
     def statistics(s_exp, t_exp, c):
         slot = lax.rem(c, DEPTH)
@@ -198,9 +202,9 @@
             stat_x_copy(c, d).start()
 
     def statistics_over_z(c):
+        await_bytes(stat_x.at[c, 1:nx], sx_recv.at[c])
         total = stat_x[c, 0]
         for d in range(1, nx):
-            stat_x_copy(c, d).wait_recv()
             total = total + stat_x[c, d]
         stat_z[c, 0] = total
         for d in range(1, nz):
@@ -208,9 +212,9 @@
 
     def gradient(s_exp, t_exp, c):
         slot = lax.rem(c, DEPTH)
+        await_bytes(stat_z.at[c, 1:nz], sz_recv.at[c])
         total = stat_z[c, 0]
         for d in range(1, nz):
-            stat_z_copy(c, d).wait_recv()
             total = total + stat_z[c, d]
         s_sum, t_sum, cross = total[0:1, :], total[1:2, :], total[2:3, :]
         loss = jnp.log(s_sum) - cross * (1.0 / STUDENT_TEMP) / t_sum
@@ -227,24 +231,22 @@
             grad_x_copy(c, d).start()
 
     def gradient_over_z(c):
-        total = grad_x[c, x]
-        for d in range(1, nx):
-            grad_x_copy(c, d).wait_recv()
-            total = total + got_x[c, d]
-        grad_z[c] = total.reshape(nz, unit_piece, width)
+        for h in range(HALVES):
+            u = c * HALVES + h
+            await_bytes(got_x.at[u, 1:nx], gx_recv.at[u])
+            total = grad_x[u, x]
+            for d in range(1, nx):
+                total = total + got_x[u, d]
+            grad_z[c, :, h] = total.reshape(nz, unit_piece, width)
         for d in range(1, nz):
             grad_z_copy(c, d).start()
 
     def finish(c):
-        parts = []
-        for h in range(HALVES):
-            u = c * HALVES + h
-            part = grad_z[u, z]
-            for d in range(1, nz):
-                grad_z_copy(u, d).wait_recv()
-                part = part + got_z[u, d]
-            parts.append(part)
-        dz = jnp.concatenate(parts, axis=0)
+        await_bytes(got_z.at[c, 1:nz], gz_recv.at[c])
+        dz = grad_z[c, z]
+        for d in range(1, nz):
+            dz = dz + got_z[c, d]
+        dz = dz.reshape(piece, width)
         image = c * nx + x
         xs = s_in[image, pl.ds(pl.multiple_of(z * piece, piece), piece), :].astype(F32)
         norm = jnp.sqrt(jnp.sum(xs * xs, axis=1, keepdims=True) + EPSILON)
@@ -257,29 +259,32 @@
         k = iota((ndp * slot_rows, piece), 1)
         pick = (((first + k) % ndp) == pos // slot_rows) & (k // ndp == pos % slot_rows)
         sent = jnp.dot(pick.astype(F32).astype(BF16), dx, preferred_element_type=F32)
-        own_dp[c] = sent.reshape(ndp, slot_rows, width)
+        own_dp[:, c] = sent.reshape(ndp, slot_rows, width)
+        got_dp[me, c] = own_dp[me, c]
+
+    def spread_dp(batch):
         for d in range(1, ndp):
-            dp_copy(c, d).start()
-        got_dp[c, me] = own_dp[c, me]
-
-    def spread_z(c):
-        for d in range(1, ndp):
-            dp_copy(c, d).wait_recv()
-        held = got_dp[c].reshape(ndp * slot_rows, width).astype(BF16)
+            dp_copy(batch, d).start()
+
+    def spread_z(batch):
+        n, at = batch
+        await_bytes(got_dp.at[0 : ndp - 1, at], dp_recv.at[n])
         pos = iota((piece, ndp * slot_rows), 0)
         k = iota((piece, ndp * slot_rows), 1)
         pick = (k // slot_rows == pos // per_res) & (k % slot_rows == pos % per_res)
-        gathered[c, x, z] = jnp.dot(
-            pick.astype(F32).astype(BF16), held, preferred_element_type=F32
-        ).astype(BF16)
+        pick = pick.astype(F32).astype(BF16)
+        for c in range(at.start, at.stop):
+            held_rows = got_dp[:, c].reshape(ndp * slot_rows, width).astype(BF16)
+            put = jnp.dot(pick, held_rows, preferred_element_type=F32)
+            gathered[c, x, z] = put.astype(BF16)
         for d in range(1, nz):
-            all_z_copy(c, d).start()
-
-    def spread_x(c):
-        for d in range(1, nz):
-            all_z_copy(c, d).wait_recv()
+            all_z_copy(batch, d).start()
+
+    def spread_x(batch):
+        n, at = batch
+        await_bytes(gathered.at[at, x, 0 : nz - 1], az_recv.at[n])
         for d in range(1, nx):
-            all_x_copy(c, d).start()
+            all_x_copy(batch, d).start()
 
     def index_rows():
         counts = counts_ref[...].astype(F32)
@@ -290,7 +295,7 @@
         )[0:1, :]
         starts = ends - counts
 
-        def index_tile(n, carry):
+        for n in range(mask_dev // tile):
             g = (n * tile + iota((tile, 1), 0)) * ndp + me
             wide = g.astype(F32)
             image = jnp.sum((wide >= ends).astype(F32), axis=1, keepdims=True).astype(jnp.int32)
@@ -298,38 +303,32 @@
             j = g - start.astype(jnp.int32)
             owner, image = image // images, image % images
             at = (image * nz + j // piece) * piece + owner * per_res + (j % piece) // ndp
-            lines = pl.ds(pl.multiple_of(n * tile, tile), tile)
+            lines = slice(n * tile, (n + 1) * tile)
             row_at[lines, :] = jnp.broadcast_to(at, (tile, 128))
             line = owner * units + (image // nx) * HALVES + (j // unit_piece) % HALVES
             lane = (image % nx) * half + (j // piece) * unit_piece + j % unit_piece
             row_key[lines, :] = jnp.broadcast_to(line * rows + lane, (tile, 128))
-            return carry
-
-        lax.fori_loop(0, mask_dev // tile, index_tile, 0)
-        grad[...] = jnp.zeros_like(grad)
-
-    def place(c):
-        for d in range(1, nx):
-            all_x_copy(c, d).wait_recv()
-        values = gathered[c].reshape(held, width)
-
-        def place_tile(n, carry):
-            lines = pl.ds(pl.multiple_of(n * tile, tile), tile)
-            at = jnp.concatenate([row_at[lines, :] - c * held] * (held // 128), axis=1)
-            pick = (iota((tile, held), 1) == at).astype(F32).astype(BF16)
+
+    def place(batch):
+        n, chunk_at = batch
+        await_bytes(gathered.at[chunk_at, 0 : nx - 1], ax_recv.at[n])
+        first, count = chunk_at.start * held, (chunk_at.stop - chunk_at.start) * held
+        values = gathered[chunk_at].reshape(count, width)
+        for i in range(mask_dev // tile):
+            lines = slice(i * tile, (i + 1) * tile)
+            at = jnp.concatenate([row_at[lines, :] - first] * (count // 128), axis=1)
+            pick = (iota((tile, count), 1) == at).astype(F32).astype(BF16)
             put = jnp.dot(pick, values, preferred_element_type=F32)
-            grad[lines, :] = (grad[lines, :].astype(F32) + put).astype(BF16)
-            return carry
-
-        lax.fori_loop(0, mask_dev // tile, place_tile, 0)
+            if chunk_at.start > 0:
+                put = put + grad[lines, :].astype(F32)
+            grad[lines, :] = put.astype(BF16)
 
     def send_losses():
         for d in range(1, ndp):
             loss_copy(d).start()
 
     def place_losses():
-        for d in range(1, ndp):
-            loss_copy(d).wait_recv()
+        await_bytes(losses.at[0 : ndp - 1], lo_recv)
         wide = losses[...].reshape(ndp * units, rows)
         high = wide.astype(BF16)
         rest = wide - high.astype(F32)
@@ -360,68 +359,54 @@
                 def _():
                     work(u // every)
 
-            @pl.when(t == DEPTH)
-            def _():
-                index_rows()
-
-            at_lag(DEPTH, functools.partial(gradient, s_exp, t_exp))
+            at_lag(0, functools.partial(statistics, s_exp, t_exp))
             at_lag(1, statistics_over_z)
-            at_lag(0, functools.partial(statistics, s_exp, t_exp))
-            at_lag(DEPTH + 2, gradient_over_z)
+            at_lag(DEPTH - 1, functools.partial(gradient, s_exp, t_exp))
+            at_lag(DEPTH + 1, gradient_over_z, HALVES)
             at_lag(DEPTH + 3, finish, HALVES)
-            at_lag(DEPTH + 4, spread_z, HALVES)
             return carry
 
-        lax.fori_loop(0, units + DEPTH, step, 0)
+        lax.fori_loop(0, units + DEPTH - 1, step, 0)
 
     pl.run_scoped(
         pipeline,
         pltpu.VMEM((DEPTH, protos, rows), F32),
         pltpu.VMEM((DEPTH, protos, rows), F32),
     )
-    def each(first, last, work):
-        def one(c, carry):
-            work(c)
-            return carry
-
-        lax.fori_loop(first, last, one, 0)
-
     last = chunks - 1
     send_losses()
+    early = [(0, slice(0, last - 1))] if last > 1 else []
+    before = (1, slice(last - 1, last))
+    final = (2, slice(last, chunks))
+    for batch in early:
+        spread_dp(batch)
+    index_rows()
+    gradient_over_z(last)
+    for batch in early:
+        spread_z(batch)
     finish(last - 1)
-    each(units - 2, units, gradient_over_z)
-    spread_z(last - 1)
-    each(0, last - 1, spread_x)
+    spread_dp(before)
+    place_losses()
+    for batch in early:
+        spread_x(batch)
     finish(last)
-    place_losses()
-    spread_x(last - 1)
-    spread_z(last)
-    each(0, last - 1, place)
-    spread_x(last)
-    each(last - 1, chunks, place)
-
-    def drain_unit(u, carry):
-        for d in range(1, nx):
-            stat_x_copy(u, d).wait_send()
-            grad_x_copy(u, d).wait_send()
-        for d in range(1, nz):
-            stat_z_copy(u, d).wait_send()
-            grad_z_copy(u, d).wait_send()
-        return carry
-
-    def drain_chunk(c, carry):
-        for d in range(1, nx):
-            all_x_copy(c, d).wait_send()
-        for d in range(1, nz):
-            all_z_copy(c, d).wait_send()
-        for d in range(1, ndp):
-            dp_copy(c, d).wait_send()
-        return carry
-
-    lax.fori_loop(0, units, drain_unit, 0)
-    lax.fori_loop(0, chunks, drain_chunk, 0)
-    for d in range(1, ndp):
-        loss_copy(d).wait_send()
+    spread_dp(final)
+    spread_z(before)
+    spread_z(final)
+    spread_x(before)
+    for batch in early:
+        place(batch)
+    spread_x(final)
+    place(before)
+    place(final)
+    await_bytes(stat_x.at[:, 1:nx], sx_send)
+    await_bytes(stat_z.at[:, 1:nz], sz_send)
+    await_bytes(got_x.at[:, 1:nx], gx_send)
+    await_bytes(got_z.at[:, 1:nz], gz_send)
+    await_bytes(got_dp.at[0 : ndp - 1], dp_send)
+    await_bytes(gathered.at[:, x, 0 : nz - 1], az_send)
+    await_bytes(gathered.at[:, 0 : nx - 1], ax_send)
+    await_bytes(losses.at[0 : ndp - 1], lo_send)
 
 
 def local(ndp, nz, nx, student_rows, teacher_rows, student_proto, teacher_proto, center, counts, order):
@@ -460,23 +445,23 @@
             pltpu.VMEM((units, nz, 4, rows), F32),
             pltpu.VMEM((units, nx, half, width), F32),
             pltpu.VMEM((units, nx, half, width), F32),
-            pltpu.VMEM((units, nz, half // nz, width), F32),
-            pltpu.VMEM((units, nz, half // nz, width), F32),
-            pltpu.VMEM((chunks, ndp, slot_rows, width), F32),
-            pltpu.VMEM((chunks, ndp, slot_rows, width), F32),
+            pltpu.VMEM((chunks, nz, HALVES, half // nz, width), F32),
+            pltpu.VMEM((chunks, nz, HALVES, half // nz, width), F32),
+            pltpu.VMEM((ndp, chunks, slot_rows, width), F32),
+            pltpu.VMEM((ndp, chunks, slot_rows, width), F32),
             pltpu.VMEM((chunks, nx, nz, piece, width), BF16),
             pltpu.VMEM((ndp, units, rows), F32),
             pltpu.VMEM((mask_dev, 128), jnp.int32),
             pltpu.VMEM((mask_dev, 128), jnp.int32),
             dma((4,)),
-            dma((units, nx)), dma((units, nx)),
-            dma((units, nz)), dma((units, nz)),
-            dma((units, nx)), dma((units, nx)),
-            dma((units, nz)), dma((units, nz)),
-            dma((chunks, ndp)), dma((chunks, ndp)),
-            dma((chunks, nz)), dma((chunks, nz)),
-            dma((chunks, nx)), dma((chunks, nx)),
-            dma((ndp,)), dma((ndp,)),
+            dma, dma((units,)),
+            dma, dma((units,)),
+            dma, dma((units,)),
+            dma, dma((chunks,)),
+            dma, dma((3,)),
+            dma, dma((3,)),
+            dma, dma((3,)),
+            dma, dma,
         ],
         compiler_params=pltpu.CompilerParams(
             collective_id=0, has_side_effects=True, vmem_limit_bytes=63 * 2**20

time: 104 us -> 81.1 us (0.78)
  Pallas kernels: 99.8 us -> 76.9 us
    pallas_call x1, Pallas kernels: 99.8 us -> 76.9 us  [local(): pl.pallas_call(functools.partial(head_kernel, dims), out_shape=(jax.Shape...]
where the time goes in v4:
time: 81.1 us; the launch traced here: 80.9 us
  Pallas kernels  76.9 us (95%)
  local copies, waits for them, and re-layouts  3.35 us (4%)
    pallas_call x1, Pallas kernels, local(): pl.pallas_call(functools.partial(head_kernel, dims), out_shape=(jax.Shape...  76.9 us
    unnamed x2, local copies, waits for them, and re-layouts  3.35 us

profile of v4, /device:TPU:1, one launch (start us, length us, event | category | flops | bytes accessed | tf_op | source)
XLA Modules:
  0.0 80.9 jit_solution(2585146745513267104)
XLA Ops:
  0.6 76.9 %proto_head.1 = (f32[1,1536]{1,0:T(1,128)}, bf16[1536,256]{1,0:T(8,128)(2,1)}) custom-call(bf16[16,256,256]{2,1,0:T(8,128)(2,1)} %refs_0_.1, bf16[16,256,256]{2,1,0:T(8,128)(2,1)} %refs_1_.1, bf16[256,4096]{1,0:T(8,128)(2,1)} %refs_2_.1, bf16[256,4096]{1,0:T(8,128)(2,1)} %refs_3_.1, f32[1,4096]{1,0:T(1,128)} %bitcast.4, s32[1,128]{1,0:T(1,128)} %bitcast.5, ...), custom_call_target="tpu_custom_call" | custom-call | tf_op jit(solution)/shard_map/proto_head/pallas_call | solution.py:428
  77.5 1.3 %copy.11 = f32[1,1536]{1,0:T(1,128)} copy(f32[1,1536]{1,0:T(1,128)} %get-tuple-element.8) | data formatting | bytes 12288
  78.8 2.1 %copy.12 = bf16[1,1536,256]{2,1,0:T(8,128)(2,1)} copy(bf16[1,1536,256]{2,1,0:T(8,128)(2,1)} %bitcast.3) | data formatting | bytes 1572864

commit v5 on v4

--- a/solution.py
+++ b/solution.py
@@ -82,8 +82,8 @@
             load.start()
 
         def spread_center(n, carry):
-            for i in range(256 // 128):
-                at = pl.ds(pl.multiple_of(n * 256 + i * 128, 128), 128)
+            for i in range(spread):
+                at = pl.ds(pl.multiple_of((n * spread + i) * 128, 128), 128)
                 row = center_ref[:, at] * (LOG2E / TEACHER_TEMP)
                 center_b[at, :] = jnp.transpose(jnp.broadcast_to(row, (128, 128)))
             return carry
@@ -115,16 +115,15 @@
                     turned[at, :] = jnp.transpose(unit)
             return carry
 
-        group = protos // 256 // chunks
-
-        def prepare(c, carry):
-            gather_chunk(c, carry)
-            return norm_tiles(c, carry)
-
-        lax.fori_loop(0, protos // 256, spread_center, 0)
-        for load in loads:
-            load.wait()
-        lax.fori_loop(0, chunks, prepare, 0)
+        spread = min(8, protos // 128)
+        group = min(4, protos // 256)
+        lax.fori_loop(0, protos // (128 * spread), spread_center, 0)
+        loads[0].wait()
+        loads[1].wait()
+        lax.fori_loop(0, chunks, gather_chunk, 0)
+        loads[2].wait()
+        loads[3].wait()
+        lax.fori_loop(0, protos // (256 * group), norm_tiles, 0)
 
     pl.run_scoped(
         prologue,
@@ -386,7 +385,6 @@
         spread_z(batch)
     finish(last - 1)
     spread_dp(before)
-    place_losses()
     for batch in early:
         spread_x(batch)
     finish(last)
@@ -396,6 +394,7 @@
     spread_x(before)
     for batch in early:
         place(batch)
+    place_losses()
     spread_x(final)
     place(before)
     place(final)
@@ -407,6 +406,17 @@
     await_bytes(gathered.at[:, x, 0 : nz - 1], az_send)
     await_bytes(gathered.at[:, 0 : nx - 1], ax_send)
     await_bytes(losses.at[0 : ndp - 1], lo_send)
+
+
+def hand_over_kernel(loss, grad, row_loss, student_grad, sem):
+    copies = [
+        pltpu.make_async_copy(loss, row_loss, sem.at[0]),
+        pltpu.make_async_copy(grad, student_grad.at[0], sem.at[1]),
+    ]
+    for each in copies:
+        each.start()
+    for each in copies:
+        each.wait()
 
 
 def local(ndp, nz, nx, student_rows, teacher_rows, student_proto, teacher_proto, center, counts, order):
@@ -468,7 +478,17 @@
         ),
         name="proto_head",
     )(student_rows, teacher_rows, student_proto, teacher_proto, center[None, :], counts[None, :], order)
-    return row_loss, grad[None]
+    return pl.pallas_call(
+        hand_over_kernel,
+        out_shape=(
+            jax.ShapeDtypeStruct((1, mask_dev), F32),
+            jax.ShapeDtypeStruct((1, mask_dev, width), BF16),
+        ),
+        in_specs=[any_spec] * 2,
+        out_specs=(any_spec, any_spec),
+        scratch_shapes=[dma((2,))],
+        name="hand_over",
+    )(row_loss, grad)
 
 
 def solution(mesh):

time: 81.1 us -> 102 us (1.26)
  Pallas kernels: 76.9 us -> 101 us
  local copies, waits for them, and re-layouts: 3.35 us -> 0 us
    pallas_call x0 -> x1, Pallas kernels: none -> 25.1 us  [local(): pl.pallas_call(hand_over_kernel, out_shape=(jax.ShapeDtypeStruct((1, mask...]
    unnamed x2 -> x0, local copies, waits for them, and re-layouts: 3.35 us -> none
    pallas_call x1, Pallas kernels: 76.9 us -> 75.6 us  [local(): pl.pallas_call(functools.partial(head_kernel, dims), out_shape=(jax.Shape...]
where the time goes in v5:
time: 102 us; the launch traced here: 101 us
  Pallas kernels  101 us (99%)
    pallas_call x1, Pallas kernels, local(): pl.pallas_call(functools.partial(head_kernel, dims), out_shape=(jax.Shape...  75.6 us
    pallas_call x1, Pallas kernels, local(): pl.pallas_call(hand_over_kernel, out_shape=(jax.ShapeDtypeStruct((1, mask...  25.1 us

profile of v5, /device:TPU:1, one launch (start us, length us, event | category | flops | bytes accessed | tf_op | source)
XLA Modules:
  0.0 101.4 jit_solution(1238758883516876304)
XLA Ops:
  0.6 75.6 %proto_head.1 = (f32[1,1536]{1,0:T(1,128)}, bf16[1536,256]{1,0:T(8,128)(2,1)}) custom-call(bf16[16,256,256]{2,1,0:T(8,128)(2,1)} %refs_0_.1, bf16[16,256,256]{2,1,0:T(8,128)(2,1)} %refs_1_.1, bf16[256,4096]{1,0:T(8,128)(2,1)} %refs_2_.1, bf16[256,4096]{1,0:T(8,128)(2,1)} %refs_3_.1, f32[1,4096]{1,0:T(1,128)} %bitcast.2, s32[1,128]{1,0:T(1,128)} %bitcast.3, ...), custom_call_target="tpu_custom_call" | custom-call | tf_op jit(solution)/shard_map/proto_head/pallas_call | solution.py:438
  76.2 25.1 %hand_over.1 = (f32[1,1536]{1,0:T(1,128)}, bf16[1,1536,256]{2,1,0:T(8,128)(2,1)}) custom-call(f32[1,1536]{1,0:T(1,128)} %get-tuple-element.4.loss, bf16[1536,256]{1,0:T(8,128)(2,1)} %get-tuple-element.5.grad), custom_call_target="tpu_custom_call" | custom-call | tf_op jit(solution)/shard_map/hand_over/pallas_call | solution.py:481

commit v6 on v5

--- a/solution.py
+++ b/solution.py
@@ -13,6 +13,7 @@
 EPSILON = 1e-06
 LOG2E = math.log2(math.e)
 X_SIZE = 4
+Z_NEAR = 4
 HALVES = 2
 DEPTH = 4
 F32 = jnp.float32
@@ -30,9 +31,9 @@
     ndp, nz, nx, images, slots, block, tile = dims
     (student_hbm, teacher_hbm, sproto_hbm, tproto_hbm, center_ref, counts_ref, order_ref,
      row_loss, grad,
-     scols, scols_t, tcols_t, center_b, s_in, s_unit, t_unit, stat_x, stat_z, grad_x, got_x,
+     scols, scols_t, tcols_t, center_b, s_in, s_unit, t_unit, stat_x, stat_z, stat_f, grad_x, got_x,
      grad_z, got_z, own_dp, got_dp, gathered, losses, row_at, row_key,
-     load_sem, sx_send, sx_recv, sz_send, sz_recv, gx_send, gx_recv, gz_send, gz_recv,
+     load_sem, sx_send, sx_recv, sz_send, sz_recv, sf_send, sf_recv, gx_send, gx_recv, gz_send, gz_recv,
      dp_send, dp_recv, az_send, az_recv, ax_send, ax_recv, lo_send, lo_recv) = refs
     chunks = images // nx
     units = chunks * HALVES
@@ -59,6 +60,12 @@
     def along_z(d):
         return (me, lax.rem(z + d, nz) * nx + x)
 
+    def along_near(d):
+        return (me, (z // Z_NEAR * Z_NEAR + lax.rem(z % Z_NEAR + d, Z_NEAR)) * nx + x)
+
+    def along_far(d):
+        return along_z(d * Z_NEAR)
+
     def along_dp(d):
         return (lax.rem(me + d, ndp), q)
 
@@ -142,7 +149,10 @@
         return copy(stat_x.at[c, 0], stat_x.at[c, d], sx_send, sx_recv.at[c], along_x(d))
 
     def stat_z_copy(c, d):
-        return copy(stat_z.at[c, 0], stat_z.at[c, d], sz_send, sz_recv.at[c], along_z(d))
+        return copy(stat_z.at[c, 0], stat_z.at[c, d], sz_send, sz_recv.at[c], along_near(d))
+
+    def stat_f_copy(c, d):
+        return copy(stat_f.at[c, 0], stat_f.at[c, d], sf_send, sf_recv.at[c], along_far(d))
 
     def grad_x_copy(c, d):
         return copy(
@@ -206,15 +216,24 @@
         for d in range(1, nx):
             total = total + stat_x[c, d]
         stat_z[c, 0] = total
-        for d in range(1, nz):
+        for d in range(1, Z_NEAR):
             stat_z_copy(c, d).start()
+
+    def statistics_over_far(c):
+        await_bytes(stat_z.at[c, 1:Z_NEAR], sz_recv.at[c])
+        total = stat_z[c, 0]
+        for d in range(1, Z_NEAR):
+            total = total + stat_z[c, d]
+        stat_f[c, 0] = total
+        for d in range(1, nz // Z_NEAR):
+            stat_f_copy(c, d).start()
 
     def gradient(s_exp, t_exp, c):
         slot = lax.rem(c, DEPTH)
-        await_bytes(stat_z.at[c, 1:nz], sz_recv.at[c])
-        total = stat_z[c, 0]
-        for d in range(1, nz):
-            total = total + stat_z[c, d]
+        await_bytes(stat_f.at[c, 1 : nz // Z_NEAR], sf_recv.at[c])
+        total = stat_f[c, 0]
+        for d in range(1, nz // Z_NEAR):
+            total = total + stat_f[c, d]
         s_sum, t_sum, cross = total[0:1, :], total[1:2, :], total[2:3, :]
         loss = jnp.log(s_sum) - cross * (1.0 / STUDENT_TEMP) / t_sum
         losses[me, pl.ds(c, 1), :] = loss
@@ -360,6 +379,7 @@
 
             at_lag(0, functools.partial(statistics, s_exp, t_exp))
             at_lag(1, statistics_over_z)
+            at_lag(2, statistics_over_far)
             at_lag(DEPTH - 1, functools.partial(gradient, s_exp, t_exp))
             at_lag(DEPTH + 1, gradient_over_z, HALVES)
             at_lag(DEPTH + 3, finish, HALVES)
@@ -399,7 +419,8 @@
     place(before)
     place(final)
     await_bytes(stat_x.at[:, 1:nx], sx_send)
-    await_bytes(stat_z.at[:, 1:nz], sz_send)
+    await_bytes(stat_z.at[:, 1:Z_NEAR], sz_send)
+    await_bytes(stat_f.at[:, 1 : nz // Z_NEAR], sf_send)
     await_bytes(got_x.at[:, 1:nx], gx_send)
     await_bytes(got_z.at[:, 1:nz], gz_send)
     await_bytes(got_dp.at[0 : ndp - 1], dp_send)
@@ -408,15 +429,9 @@
     await_bytes(losses.at[0 : ndp - 1], lo_send)
 
 
-def hand_over_kernel(loss, grad, row_loss, student_grad, sem):
-    copies = [
-        pltpu.make_async_copy(loss, row_loss, sem.at[0]),
-        pltpu.make_async_copy(grad, student_grad.at[0], sem.at[1]),
-    ]
-    for each in copies:
-        each.start()
-    for each in copies:
-        each.wait()
+def hand_over_kernel(loss, grad, row_loss, student_grad):
+    row_loss[...] = loss[...]
+    student_grad[0] = grad[...]
 
 
 def local(ndp, nz, nx, student_rows, teacher_rows, student_proto, teacher_proto, center, counts, order):
@@ -452,7 +467,8 @@
             pltpu.VMEM((units, nx, half, width), BF16),
             pltpu.VMEM((units, nx, half, width), BF16),
             pltpu.VMEM((units, nx, 4, rows), F32),
-            pltpu.VMEM((units, nz, 4, rows), F32),
+            pltpu.VMEM((units, Z_NEAR, 4, rows), F32),
+            pltpu.VMEM((units, nz // Z_NEAR, 4, rows), F32),
             pltpu.VMEM((units, nx, half, width), F32),
             pltpu.VMEM((units, nx, half, width), F32),
             pltpu.VMEM((chunks, nz, HALVES, half // nz, width), F32),
@@ -464,6 +480,7 @@
             pltpu.VMEM((mask_dev, 128), jnp.int32),
             pltpu.VMEM((mask_dev, 128), jnp.int32),
             dma((4,)),
+            dma, dma((units,)),
             dma, dma((units,)),
             dma, dma((units,)),
             dma, dma((units,)),
@@ -484,9 +501,8 @@
             jax.ShapeDtypeStruct((1, mask_dev), F32),
             jax.ShapeDtypeStruct((1, mask_dev, width), BF16),
         ),
-        in_specs=[any_spec] * 2,
-        out_specs=(any_spec, any_spec),
-        scratch_shapes=[dma((2,))],
+        in_specs=[vmem] * 2,
+        out_specs=(vmem, vmem),
         name="hand_over",
     )(row_loss, grad)
 

time: 102 us -> 86.8 us (0.85)
  Pallas kernels: 101 us -> 85.9 us
    pallas_call x1, Pallas kernels: 25.1 us -> 2.08 us  [local(): pl.pallas_call(hand_over_kernel, out_shape=(jax.ShapeDtypeStruct((1, mask...]
    pallas_call x1, Pallas kernels: 75.6 us -> 83.9 us  [local(): pl.pallas_call(functools.partial(head_kernel, dims), out_shape=(jax.Shape...]
where the time goes in v6:
time: 86.8 us; the launch traced here: 86.6 us
  Pallas kernels  85.9 us (99%)
    pallas_call x1, Pallas kernels, local(): pl.pallas_call(functools.partial(head_kernel, dims), out_shape=(jax.Shape...  83.9 us
    pallas_call x1, Pallas kernels, local(): pl.pallas_call(hand_over_kernel, out_shape=(jax.ShapeDtypeStruct((1, mask...  2.08 us

profile of v6, /device:TPU:1, one launch (start us, length us, event | category | flops | bytes accessed | tf_op | source)
XLA Modules:
  0.0 86.6 jit_solution(11215955164191437143)
XLA Ops:
  0.6 83.9 %proto_head.1 = (f32[1,1536]{1,0:T(1,128)}, bf16[1536,256]{1,0:T(8,128)(2,1)}) custom-call(bf16[16,256,256]{2,1,0:T(8,128)(2,1)} %refs_0_.1, bf16[16,256,256]{2,1,0:T(8,128)(2,1)} %refs_1_.1, bf16[256,4096]{1,0:T(8,128)(2,1)} %refs_2_.1, bf16[256,4096]{1,0:T(8,128)(2,1)} %refs_3_.1, f32[1,4096]{1,0:T(1,128)} %bitcast.2, s32[1,128]{1,0:T(1,128)} %bitcast.3, ...), custom_call_target="tpu_custom_call" | custom-call | tf_op jit(solution)/shard_map/proto_head/pallas_call | solution.py:453
  84.5 2.1 %hand_over.1 = (f32[1,1536]{1,0:T(1,128)}, bf16[1,1536,256]{2,1,0:T(8,128)(2,1)}) custom-call(f32[1,1536]{1,0:T(1,128)} %get-tuple-element.4.loss, bf16[1536,256]{1,0:T(8,128)(2,1)} %get-tuple-element.5.grad), custom_call_target="tpu_custom_call" | custom-call | tf_op jit(solution)/shard_map/hand_over/pallas_call | solution.py:498

commit v7 on v5

--- a/solution.py
+++ b/solution.py
@@ -408,15 +408,9 @@
     await_bytes(losses.at[0 : ndp - 1], lo_send)
 
 
-def hand_over_kernel(loss, grad, row_loss, student_grad, sem):
-    copies = [
-        pltpu.make_async_copy(loss, row_loss, sem.at[0]),
-        pltpu.make_async_copy(grad, student_grad.at[0], sem.at[1]),
-    ]
-    for each in copies:
-        each.start()
-    for each in copies:
-        each.wait()
+def hand_over_kernel(loss, grad, row_loss, student_grad):
+    row_loss[...] = loss[...]
+    student_grad[0] = grad[...]
 
 
 def local(ndp, nz, nx, student_rows, teacher_rows, student_proto, teacher_proto, center, counts, order):
@@ -484,9 +478,8 @@
             jax.ShapeDtypeStruct((1, mask_dev), F32),
             jax.ShapeDtypeStruct((1, mask_dev, width), BF16),
         ),
-        in_specs=[any_spec] * 2,
-        out_specs=(any_spec, any_spec),
-        scratch_shapes=[dma((2,))],
+        in_specs=[vmem] * 2,
+        out_specs=(vmem, vmem),
         name="hand_over",
     )(row_loss, grad)
 

time: 102 us -> 79.2 us (0.78)
  Pallas kernels: 101 us -> 77.7 us
    pallas_call x1, Pallas kernels: 25.1 us -> 2.08 us  [local(): pl.pallas_call(hand_over_kernel, out_shape=(jax.ShapeDtypeStruct((1, mask...]
where the time goes in v7:
time: 79.2 us; the launch traced here: 78.3 us
  Pallas kernels  77.7 us (98%)
    pallas_call x1, Pallas kernels, local(): pl.pallas_call(functools.partial(head_kernel, dims), out_shape=(jax.Shape...  75.6 us
    pallas_call x1, Pallas kernels, local(): pl.pallas_call(hand_over_kernel, out_shape=(jax.ShapeDtypeStruct((1, mask...  2.08 us

profile of v7, /device:TPU:1, one launch (start us, length us, event | category | flops | bytes accessed | tf_op | source)
XLA Modules:
  0.0 78.3 jit_solution(17759072190430891173)
XLA Ops:
  0.6 75.6 %proto_head.1 = (f32[1,1536]{1,0:T(1,128)}, bf16[1536,256]{1,0:T(8,128)(2,1)}) custom-call(bf16[16,256,256]{2,1,0:T(8,128)(2,1)} %refs_0_.1, bf16[16,256,256]{2,1,0:T(8,128)(2,1)} %refs_1_.1, bf16[256,4096]{1,0:T(8,128)(2,1)} %refs_2_.1, bf16[256,4096]{1,0:T(8,128)(2,1)} %refs_3_.1, f32[1,4096]{1,0:T(1,128)} %bitcast.2, s32[1,128]{1,0:T(1,128)} %bitcast.3, ...), custom_call_target="tpu_custom_call" | custom-call | tf_op jit(solution)/shard_map/proto_head/pallas_call | solution.py:432
  76.2 2.1 %hand_over.1 = (f32[1,1536]{1,0:T(1,128)}, bf16[1,1536,256]{2,1,0:T(8,128)(2,1)}) custom-call(f32[1,1536]{1,0:T(1,128)} %get-tuple-element.4.loss, bf16[1536,256]{1,0:T(8,128)(2,1)} %get-tuple-element.5.grad), custom_call_target="tpu_custom_call" | custom-call | tf_op jit(solution)/shard_map/hand_over/pallas_call | solution.py:475

commit v8 on v7

--- a/solution.py
+++ b/solution.py
@@ -394,8 +394,8 @@
     spread_x(before)
     for batch in early:
         place(batch)
+    spread_x(final)
     place_losses()
-    spread_x(final)
     place(before)
     place(final)
     await_bytes(stat_x.at[:, 1:nx], sx_send)

time: 79.2 us -> 78.6 us (level)
  no operation moved by 1% of the time
where the time goes in v8:
time: 78.6 us; the launch traced here: 78.3 us
  Pallas kernels  77.7 us (99%)
    pallas_call x1, Pallas kernels, local(): pl.pallas_call(functools.partial(head_kernel, dims), out_shape=(jax.Shape...  75.6 us
    pallas_call x1, Pallas kernels, local(): pl.pallas_call(hand_over_kernel, out_shape=(jax.ShapeDtypeStruct((1, mask...  2.08 us

profile of v8, /device:TPU:1, one launch (start us, length us, event | category | flops | bytes accessed | tf_op | source)
XLA Modules:
  0.0 78.3 jit_solution(8627449493318175603)
XLA Ops:
  0.6 75.6 %proto_head.1 = (f32[1,1536]{1,0:T(1,128)}, bf16[1536,256]{1,0:T(8,128)(2,1)}) custom-call(bf16[16,256,256]{2,1,0:T(8,128)(2,1)} %refs_0_.1, bf16[16,256,256]{2,1,0:T(8,128)(2,1)} %refs_1_.1, bf16[256,4096]{1,0:T(8,128)(2,1)} %refs_2_.1, bf16[256,4096]{1,0:T(8,128)(2,1)} %refs_3_.1, f32[1,4096]{1,0:T(1,128)} %bitcast.2, s32[1,128]{1,0:T(1,128)} %bitcast.3, ...), custom_call_target="tpu_custom_call" | custom-call | tf_op jit(solution)/shard_map/proto_head/pallas_call | solution.py:432
  76.2 2.1 %hand_over.1 = (f32[1,1536]{1,0:T(1,128)}, bf16[1,1536,256]{2,1,0:T(8,128)(2,1)}) custom-call(f32[1,1536]{1,0:T(1,128)} %get-tuple-element.4.loss, bf16[1536,256]{1,0:T(8,128)(2,1)} %get-tuple-element.5.grad), custom_call_target="tpu_custom_call" | custom-call | tf_op jit(solution)/shard_map/hand_over/pallas_call | solution.py:475
